TPU v7x, 512 devices: a whole 4x8x8 slice. The times are simulated.
512 devices in a mesh: dp: 16 (over x, z_hi, core), expert: 32 (over z_lo, y).
Axes of the slice: x: 4, y: 8, z: 8 (z_hi: 2, z_lo: 4; z = z_hi * 4 + z_lo), core: 2. Of those that a mesh axis runs over, the one named last changes fastest.
Arguments:
- tokens_in: bfloat16 [65536, 4096], P(('dp', 'expert')), may hold values from -6 to 6
- out_grad: bfloat16 [65536, 4096], P(('dp', 'expert')), may hold values from -6 to 6
- routes: int32 [65536, 2], P(('dp', 'expert')), may hold values from 0 to 31, as said below
- router_probs: float32 [65536, 2], P(('dp', 'expert')), may hold values from 0.1 to 1
- gate_up: bfloat16 [2, 4096, 4096], P(None, 'expert', 'dp'), may hold values from -0.09375 to 0.09375
- down_proj: bfloat16 [4096, 4096], P('expert', 'dp'), may hold values from -0.09375 to 0.09375
Outputs:
- in_grad: bfloat16 [65536, 4096], P(('dp', 'expert'))
- grad_gate_up: float32 [2, 4096, 4096], P(None, 'expert', 'dp')
- grad_down: float32 [4096, 4096], P('expert', 'dp')
Inputs may be any that keep to these rules, and one draw needn't show every extreme that they name: `routes`: each row names two different experts. Expert 0 is the expert in the window: each token names it at most once, the tokens of one device (an aligned block of 128 rows) name it at most 8 times, and on every device of one index of dp (which index varies by draw) exactly 8 times; devices of the other indices of dp may hold fewer.
All inputs are finite; a program needn't handle non-finite values.
Results may differ from a plain program's by a relative error of at most 0.015.
Values may be sent and summed in bfloat16 or wider, within the bound.
A program may use at most 64 MiB of HBM per device.

v0:
```python
import jax
import jax.numpy as jnp
from jax import lax
from jax.sharding import PartitionSpec as P


def on_device(tokens_in, out_grad, routes, router_probs, gate_up, down_proj):
    chosen = routes == 0
    weight = jnp.sum(jnp.where(chosen, router_probs, jnp.float32(0.0)), axis=1)
    member = jnp.any(chosen, axis=1)
    slot_count = tokens_in.shape[0] // 16
    position = jnp.cumsum(member.astype(jnp.int32)) - 1
    placed = (position[None, :] == jnp.arange(slot_count, dtype=jnp.int32)[:, None]) & member[
        None, :
    ]
    picker = placed.astype(jnp.bfloat16)
    scaled = (weight[:, None] * out_grad.astype(jnp.float32)).astype(jnp.bfloat16)
    send_rows = jnp.dot(picker, tokens_in, preferred_element_type=jnp.float32).astype(jnp.bfloat16)
    send_grad = jnp.dot(picker, scaled, preferred_element_type=jnp.float32).astype(jnp.bfloat16)
    dispatched_rows, dispatched_grad = (
        lax.all_gather(send_rows, "expert", axis=0, tiled=True),
        lax.all_gather(send_grad, "expert", axis=0, tiled=True),
    )
    full_pair, full_down = (
        lax.all_gather(gate_up, "dp", axis=2, tiled=True),
        lax.all_gather(down_proj, "dp", axis=1, tiled=True),
    )
    projected = jnp.einsum(
        "rd,kud->kru", dispatched_rows, full_pair, preferred_element_type=jnp.float32
    )
    gate_pre = projected[0]
    up_pre = projected[1]
    hidden_grad = jnp.einsum(
        "rd,ud->ru", dispatched_grad, full_down, preferred_element_type=jnp.float32
    )
    sigmoid_gate = jax.nn.sigmoid(gate_pre)
    activated = gate_pre * sigmoid_gate
    hidden = (activated * up_pre).astype(jnp.bfloat16)
    up_grad = (hidden_grad * activated).astype(jnp.bfloat16)
    gate_grad = (
        hidden_grad * up_pre * sigmoid_gate * (1.0 + gate_pre * (1.0 - sigmoid_gate))
    ).astype(jnp.bfloat16)
    pair_grad = jnp.stack([gate_grad, up_grad])
    partial_rows = jnp.einsum(
        "kru,kud->rd", pair_grad, full_pair, preferred_element_type=jnp.float32
    ).astype(jnp.bfloat16)
    returned = lax.all_to_all(partial_rows, "expert", split_axis=0, concat_axis=0, tiled=True)
    owners = lax.axis_size("expert")
    summed = jnp.sum(returned.reshape(owners, slot_count, -1).astype(jnp.float32), axis=0)
    token_grad = jnp.dot(
        placed.astype(jnp.float32).T, summed, precision=lax.Precision.HIGHEST
    ).astype(jnp.bfloat16)
    pair_term = jnp.einsum(
        "kru,rd->kud", pair_grad, dispatched_rows, preferred_element_type=jnp.float32
    )
    down_term = jnp.einsum("ru,rd->ud", hidden, dispatched_grad, preferred_element_type=jnp.float32)
    weight_pair, weight_down = (
        lax.psum_scatter(
            pair_term.astype(jnp.bfloat16), "dp", scatter_dimension=2, tiled=True
        ).astype(jnp.float32),
        lax.psum_scatter(
            down_term.astype(jnp.bfloat16), "dp", scatter_dimension=1, tiled=True
        ).astype(jnp.float32),
    )
    return (token_grad, weight_pair, weight_down)


def solution(mesh):
    in_specs = (
        P(("dp", "expert"), None),
        P(("dp", "expert"), None),
        P(("dp", "expert"), None),
        P(("dp", "expert"), None),
        P(None, "expert", "dp"),
        P("expert", "dp"),
    )
    out_specs = (P(("dp", "expert"), None), P(None, "expert", "dp"), P("expert", "dp"))
    return jax.shard_map(
        on_device, mesh=mesh, in_specs=in_specs, out_specs=out_specs, check_vma=False
    )
```

profile of v0, /device:TPU:1, one launch (start us, length us, event | category | flops | bytes accessed | tf_op | source)
XLA Modules:
  0.0 662.9 jit_solution(10199664705968635727)
XLA Ops:
  7.2 0.0 copy-start
  7.2 0.0 all-gather.11.cloned.1.call-start
  7.2 0.7 all-gather.11.cloned.1.call-update
  7.9 0.0 all-gather.9.cloned.1.call-start
  8.0 0.7 fusion.23
  8.7 0.1 copy.11
  8.8 0.2 reduce-window.8
  9.0 0.1 add_reduce_fusion
  9.1 0.0 copy-done
  9.1 0.9 convolution_convert_fusion.3
  10.0 0.0 all-gather.9.cloned.1.call-update
  10.0 0.0 all-gather.5.cloned.1.call-start
  10.0 0.7 select_reduce_fusion
  10.7 2.2 convolution_convert_fusion.4
  13.0 0.0 all-gather.5.cloned.1.call-update
  13.0 0.0 all-gather.7.cloned.1.call-start
  13.0 0.5 all-gather.7.cloned.1.call-update
  13.6 0.0 reduce-scatter.5.cloned.1.call-start
  13.6 72.5 %all-gather.11.cloned.1.call-done = bf16[2,128,4096]{2,1,0:T(8,128)(2,1)} async-done(((bf16[2,128,256]{2,1,0:T(8,128)(2,1)}), bf16[2,128,4096]{2,1,0:T(8,128)(2,1)}) %all-gather.11.cloned.1.call-update) | async-done | bytes 2097168 | tf_op jit(solution)/shard_map/all_gather | solution.py:25
  86.1 132.4 %all-gather.9.cloned.1.call-done = bf16[256,4096]{1,0:T(8,128)(2,1)} async-done(((bf16[8,4096]{1,0:T(8,128)(2,1)}), bf16[256,4096]{1,0:T(8,128)(2,1)}) %all-gather.9.cloned.1.call-update) | async-done | bytes 2097168 | tf_op jit(solution)/shard_map/all_gather | solution.py:21
  218.5 3.0 fusion.5
  221.5 149.8 %all-gather.5.cloned.1.call-done = bf16[256,4096]{1,0:T(8,128)(2,1)} async-done(((bf16[8,4096]{1,0:T(8,128)(2,1)}), bf16[256,4096]{1,0:T(8,128)(2,1)}) %all-gather.5.cloned.1.call-update) | async-done | bytes 2097168 | tf_op jit(solution)/shard_map/all_gather | solution.py:22
  371.3 3.1 convolution_convert_fusion.1
  374.4 0.0 reduce-scatter.5.cloned.1.call-update
  374.4 0.0 copy-start.1
  374.4 77.9 %all-gather.7.cloned.1.call-done = bf16[128,4096]{1,0:T(8,128)(2,1)} async-done(((bf16[128,256]{1,0:T(8,128)(2,1)}), bf16[128,4096]{1,0:T(8,128)(2,1)}) %all-gather.7.cloned.1.call-update) | async-done | bytes 1048592 | tf_op jit(solution)/shard_map/all_gather | solution.py:26
  452.3 2.6 fusion.11
  454.8 0.0 copy-done.1
  454.9 2.0 fusion.1
  456.9 0.0 copy-start.2
  456.9 7.5 %all-to-all-start = ((bf16[32,8,4096]{2,1,0:T(8,128)(2,1)}), bf16[32,8,4096]{2,1,0:T(8,128)(2,1)}, u32[]{:S(2)}, u32[]{:S(2)}) async-start(bf16[32,8,4096]{2,1,0:T(8,128)(2,1)} %fusion.1), calls=%async_computation | async-start | bytes 4194304 | tf_op jit(solution)/shard_map/all_to_all | solution.py:47
  464.4 0.0 reduce-scatter.3.cloned.1.call-start
  464.5 0.0 copy-done.2
  464.5 2.1 convolution_convert_fusion
  466.6 0.0 reduce-scatter.3.cloned.1.call-update
  466.6 85.7 %reduce-scatter.5.cloned.1.call-done = bf16[128,256]{1,0:T(8,128)(2,1)} async-done(((bf16[128,4096]{1,0:T(8,128)(2,1)}), bf16[128,256]{1,0:T(8,128)(2,1)}) %reduce-scatter.5.cloned.1.call-update) | async-done | bytes 65552 | tf_op jit(solution)/shard_map/reduce_scatter | solution.py:61
  552.3 1.5 convert_element_type.74
  553.8 96.7 %reduce-scatter.3.cloned.1.call-done = bf16[2,128,256]{2,1,0:T(8,128)(2,1)} async-done(((bf16[2,128,4096]{2,1,0:T(8,128)(2,1)}), bf16[2,128,256]{2,1,0:T(8,128)(2,1)}) %reduce-scatter.3.cloned.1.call-update) | async-done | bytes 131088 | tf_op jit(solution)/shard_map/reduce_scatter | solution.py:58
  650.5 1.6 convert_element_type.71
  652.1 0.0 all-to-all-done
  652.1 1.9 convert_reduce_fusion
  654.0 2.0 convolution_convert_fusion.2
  (1 shorter events, 0.0 us)
Async XLA Ops:
  7.2 1.9 copy-start
  7.2 78.9 %all-gather.11.cloned.1.call-start = ((), (), s32[]{:S(2)}) async-start(), calls=%async_computation.6 | async-start | bytes 2228224 | tf_op jit(solution)/shard_map/all_gather | solution.py:25
  7.9 210.6 %all-gather.9.cloned.1.call-start = ((), (), s32[]{:S(2)}) async-start(), calls=%async_computation.5 | async-start | bytes 2162688 | tf_op jit(solution)/shard_map/all_gather | solution.py:21
  10.0 361.3 %all-gather.5.cloned.1.call-start = ((), (), s32[]{:S(2)}) async-start(), calls=%async_computation.3 | async-start | bytes 2162688 | tf_op jit(solution)/shard_map/all_gather | solution.py:22
  13.0 439.3 %all-gather.7.cloned.1.call-start = ((), (), s32[]{:S(2)}) async-start(), calls=%async_computation.4 | async-start | bytes 1114112 | tf_op jit(solution)/shard_map/all_gather | solution.py:26
  13.6 538.8 %reduce-scatter.5.cloned.1.call-start = ((), (), s32[]{:S(2)}) async-start(), calls=%async_computation.8 | async-start | bytes 1114112 | tf_op jit(solution)/shard_map/reduce_scatter | solution.py:61
  374.4 80.5 %copy-start.1 = (bf16[2,128,4096]{2,1,0:T(8,128)(2,1)S(1)}, bf16[2,128,4096]{2,1,0:T(8,128)(2,1)}, u32[]{:S(2)}) copy-start(bf16[2,128,4096]{2,1,0:T(8,128)(2,1)} %all-gather.11.cloned.1.call-done) | copy-start | bytes 6291460
  456.9 7.6 %copy-start.2 = (bf16[256,4096]{1,0:T(8,128)(2,1)S(1)}, bf16[256,4096]{1,0:T(8,128)(2,1)}, u32[]{:S(2)}) copy-start(bf16[256,4096]{1,0:T(8,128)(2,1)} %all-gather.9.cloned.1.call-done) | copy-start | bytes 6291460
  456.9 195.2 %all-to-all-start = ((bf16[32,8,4096]{2,1,0:T(8,128)(2,1)}), bf16[32,8,4096]{2,1,0:T(8,128)(2,1)}, u32[]{:S(2)}, u32[]{:S(2)}) async-start(bf16[32,8,4096]{2,1,0:T(8,128)(2,1)} %fusion.1), calls=%async_computation | async-start | bytes 4194304 | tf_op jit(solution)/shard_map/all_to_all | solution.py:47
  464.4 186.1 %reduce-scatter.3.cloned.1.call-start = ((), (), s32[]{:S(2)}) async-start(), calls=%async_computation.7 | async-start | bytes 2228224 | tf_op jit(solution)/shard_map/reduce_scatter | solution.py:58
Sparse Core Ops, SparseCore 0:
  11.1 74.8 all-gather.10
  88.7 129.7 all-gather.8
  221.2 150.0 all-gather.4
  374.3 77.9 all-gather.6
  457.4 94.8 reduce-scatter.4
  557.7 92.7 reduce-scatter.2
where the time goes:
time: 664 us; the launch traced here: 663 us
  waiting for transfers between devices  616 us (93%)
  matrix products  17.8 us (3%)
  between operations  14.2 us (2%)
  starting transfers between devices  7.78 us (1%)
  other arithmetic  6.71 us (1%)
    all_gather x1, waiting for transfers between devices, on_device(): lax.all_gather(send_grad, 'expert', axis=0, tiled=True)  150 us
    all_gather x1, waiting for transfers between devices, on_device(): lax.all_gather(send_rows, 'expert', axis=0, tiled=True)  132 us
    reduce_scatter x1, waiting for transfers between devices, on_device(): lax.psum_scatter(pair_term.astype(jnp.bfloat16), 'dp', scatter_dimension=...  96.7 us
    reduce_scatter x1, waiting for transfers between devices, on_device(): lax.psum_scatter(down_term.astype(jnp.bfloat16), 'dp', scatter_dimension=...  85.7 us
    all_gather x1, waiting for transfers between devices, on_device(): lax.all_gather(down_proj, 'dp', axis=1, tiled=True)  77.9 us
    all_gather x1, waiting for transfers between devices, on_device(): lax.all_gather(gate_up, 'dp', axis=2, tiled=True)  72.5 us
  transfers between devices with their start and end apart: 7, of which 6 were waited for; matrix products, arithmetic and copies ran while one was open for 3% of the time, Pallas kernels for 0%

commit v1 on v0

v1 whole, which is shorter than its diff:
```python
import jax
import jax.numpy as jnp
from jax import lax
from jax.experimental import pallas as pl
from jax.experimental.pallas import tpu as pltpu
from jax.sharding import PartitionSpec as P

MESH = pl.DeviceIdType.MESH
F32, BF16 = jnp.float32, jnp.bfloat16
NX, NY, NZ = 4, 8, 4
D = 4096
CAP = 8
COLS = 256
UNITS = 128
HALF = 3 * UNITS // 2


class Sems:
    def __init__(self, send, recv):
        self.send, self.recv, self.used = send, recv, 0

    def take(self, n=1):
        at = self.used
        self.used += n
        return at


def kernel(
    tok_hbm, og_hbm, routes, probs, gu_hbm, dn_hbm,
    out_tok, out_gu, out_dn,
    tok, og, G, W, A_t, dH, R, yrecv, zrecv, T, crecv, xrecv, zhrecv, zhsend,
    load_sem, send_sem, recv_sem,
):
    dp, ex = lax.axis_index("dp"), lax.axis_index("expert")
    x, zh, c = dp // 4, (dp // 2) % 2, dp % 2
    zl, y = ex // NY, ex % NY

    def at(x=x, zh=zh, c=c, zl=zl, y=y):
        return ((x * 2 + zh) * 2 + c, zl * NY + y)

    right, left = at(x=(x + 1) % NX), at(x=(x + NX - 1) % NX)
    north, south = at(y=(y + 1) % NY), at(y=(y + NY - 1) % NY)
    other_core, other_run = at(c=1 - c), at(zh=1 - zh)
    in_run = [at(zl=(zl + j) % NZ) for j in range(1, NZ)]

    barrier = pltpu.get_barrier_semaphore()
    peers = [right, left, north, south, other_core, other_run] + in_run
    for peer in peers:
        pl.semaphore_signal(barrier, inc=1, device_id=peer, device_id_type=MESH)

    def cols(i):
        return pl.ds(pl.multiple_of(i * COLS, COLS), COLS)

    mine = cols(dp)
    loads = [
        pltpu.make_async_copy(tok_hbm, tok, load_sem.at[0]),
        pltpu.make_async_copy(og_hbm, og, load_sem.at[1]),
        pltpu.make_async_copy(gu_hbm.at[0], W.at[pl.ds(0, UNITS), mine], load_sem.at[2]),
        pltpu.make_async_copy(gu_hbm.at[1], W.at[pl.ds(UNITS, UNITS), mine], load_sem.at[3]),
        pltpu.make_async_copy(dn_hbm, W.at[pl.ds(2 * UNITS, UNITS), mine], load_sem.at[4]),
    ]
    for load in loads:
        load.start()

    n_tok = tok.shape[0]
    chosen = routes[...] == 0
    weight = jnp.sum(jnp.where(chosen, probs[...], 0.0), axis=1, keepdims=True)
    member = jnp.sum(jnp.where(chosen, 1.0, 0.0), axis=1, keepdims=True)
    member_l = jnp.broadcast_to(member, (n_tok, n_tok)).T[: 2 * CAP]
    weight_l = jnp.broadcast_to(weight, (n_tok, n_tok)).T[: 2 * CAP]
    before = lax.broadcasted_iota(jnp.int32, (n_tok, n_tok), 0)
    upto = lax.broadcasted_iota(jnp.int32, (n_tok, n_tok), 1)
    prefix = jnp.where(before <= upto, 1.0, 0.0).astype(BF16)
    position = jnp.dot(member_l.astype(BF16), prefix, preferred_element_type=F32)
    slot = (lax.broadcasted_iota(jnp.int32, (2 * CAP, n_tok), 0) % CAP).astype(F32)
    picker = jnp.where((position - 1.0 == slot) & (member_l > 0.5), 1.0, 0.0)
    slot_weight = jnp.sum(picker * weight_l, axis=1, keepdims=True)
    picker_b = picker.astype(BF16)
    own_block = y * NZ + zl
    for load in loads:
        load.wait()
    x_rows = jnp.dot(picker_b, tok[...], preferred_element_type=F32)
    g_rows = jnp.dot(picker_b, og[...], preferred_element_type=F32)
    e_rows = slot_weight * g_rows
    G[own_block] = jnp.concatenate([x_rows[:CAP], e_rows[CAP:]], axis=0).astype(BF16)

    pl.semaphore_wait(barrier, len(peers))

    sems = Sems(send_sem, recv_sem)
    sent = []

    def copy(src, dst, device, k):
        return pltpu.make_async_remote_copy(
            src_ref=src,
            dst_ref=dst,
            send_sem=send_sem.at[k],
            recv_sem=recv_sem.at[k],
            device_id=device,
            device_id_type=MESH,
        )

    def go(src, dst, device, k=None):
        one = copy(src, dst, device, sems.take() if k is None else k)
        one.start()
        sent.append(one)
        return one

    upper = zl // 2
    m = zl * (1 - upper) + (3 - zl) * upper
    order = [b * (1 - upper) + (3 - b) * upper for b in (m, 1 - m, 2, 3)]

    z_up, z_down = sems.take(NZ), sems.take(NZ)
    z_sent = []

    def z_copy(zs, up):
        ref = G.at[y * NZ + zs]
        return pltpu.make_async_remote_copy(
            src_ref=ref,
            dst_ref=ref,
            send_sem=send_sem.at[(z_up if up else z_down) + zs],
            recv_sem=recv_sem.at[z_up + zs],
            device_id=at(zl=(zl + (1 if up else NZ - 1)) % NZ),
            device_id_type=MESH,
        )

    def z_forward(zs):
        @pl.when((zs <= zl) & (zl < NZ - 1))
        def _():
            z_copy(zs, True).start()

        @pl.when((zs >= zl) & (zl > 0))
        def _():
            z_copy(zs, False).start()

        z_sent.append(zs)

    def hops(k, plus):
        return 4 if (k in (0, 3)) == plus else 3

    y_live = {}

    def y_send(k, h, plus):
        src_y = (y + (NY - h + 1 if plus else h - 1)) % NY
        ref = G.at[src_y * NZ + order[k]]
        y_live[k, h, plus] = go(ref, ref, north if plus else south)

    def y_step(k, h):
        for plus in (True, False):
            if 1 <= h - 1 <= hops(k, plus):
                y_live[k, h - 1, plus].wait_recv()
            if h <= hops(k, plus):
                y_send(k, h, plus)

    def block_of(xx, zz, cc):
        return (xx * 2 + zz) * 2 + cc

    def w_ref(xx, zz, rows=pl.ds(0, 3 * UNITS), cc=c):
        return W.at[rows, cols(block_of(xx, zz, cc))]

    lo, hi = pl.ds(0, HALF), pl.ds(HALF, HALF)
    x1, x2, x3 = (x + 1) % NX, (x + 2) % NX, (x + 3) % NX
    to_core = []

    def w_core(xx, zz):
        to_core.append(go(w_ref(xx, zz), w_ref(xx, zz), other_core))

    def w_hop1(zz):
        ref = w_ref(x, zz)
        return go(ref, ref, right), go(ref, ref, left)

    def w_hop2(zz, first):
        first[0].wait_recv()
        a = go(w_ref(x3, zz, lo), w_ref(x3, zz, lo), right)
        first[1].wait_recv()
        b = go(w_ref(x1, zz, hi), w_ref(x1, zz, hi), left)
        w_core(x3, zz)
        w_core(x1, zz)
        return a, b

    def w_last(zz, second):
        second[0].wait_recv()
        second[1].wait_recv()
        w_core(x2, zz)

    z_forward(order[0])
    y_step(0, 1)
    w_run = go(w_ref(x, zh), w_ref(x, zh), other_run)
    first_a = w_hop1(zh)
    w_core(x, zh)
    for t in range(1, 8):
        for k in range(4):
            h = t - k + 1
            if h == 1:
                z_copy(order[k], True).wait_recv()
                z_forward(order[k])
            if 1 <= h <= 5:
                y_step(k, h)
        if t == 1:
            second_a = w_hop2(zh, first_a)
        if t == 3:
            w_run.wait_recv()
            first_b = w_hop1(1 - zh)
            w_core(x, 1 - zh)
            w_last(zh, second_a)
        if t == 5:
            second_b = w_hop2(1 - zh, first_b)
        if t == 7:
            w_last(1 - zh, second_b)
    for one in to_core:
        one.wait_recv()

    for half in range(2):
        g = G[pl.ds(half * 16, 16)].reshape(256, D)
        pre = lax.dot_general(g, W[...], (((1,), (1,)), ((), ())), preferred_element_type=F32)
        pre = pre.reshape(16, 2 * CAP, 3 * UNITS)
        gate_pre = pre[:, :CAP, :UNITS]
        up_pre = pre[:, :CAP, UNITS : 2 * UNITS]
        hidden_grad = pre[:, CAP:, 2 * UNITS :]
        sig = 1.0 / (1.0 + jnp.exp(-gate_pre))
        activated = gate_pre * sig
        hidden = activated * up_pre
        up_grad = hidden_grad * activated
        gate_grad = hidden_grad * up_pre * sig * (1.0 + gate_pre * (1.0 - sig))
        zero = jnp.zeros_like(hidden)
        a = jnp.concatenate(
            [
                jnp.concatenate([gate_grad, up_grad, zero], axis=2),
                jnp.concatenate([zero, zero, hidden], axis=2),
            ],
            axis=1,
        ).reshape(256, 3 * UNITS)
        A_t[:, pl.ds(half * 256, 256)] = a.T.astype(BF16)
        grads = jnp.concatenate([gate_grad, up_grad], axis=2).reshape(128, 2 * UNITS)
        dH[pl.ds(half * 128, 128)] = grads.astype(BF16)

    def weight_grad(i):
        g = G[:, :, cols(i)].reshape(512, COLS)
        T[i] = jnp.dot(A_t[...], g, preferred_element_type=F32).astype(BF16)

    x_order = [x2, x1, x3, x]
    core_copies = []
    for n, xx in enumerate(x_order):
        for zz in range(2):
            i = block_of(xx, zz, 1 - c)
            weight_grad(i)
            core_copies.append(go(T.at[i], crecv.at[2 * n + zz], other_core))

    WIDE = 512
    for j in range(D // 2 // WIDE):
        parts = []
        for base in (0, D // 2):
            w = W[pl.ds(0, 2 * UNITS), pl.ds(base + j * WIDE, WIDE)]
            part = jnp.dot(dH[...], w, preferred_element_type=F32)
            parts.append(part.reshape(NY * NZ, CAP, WIDE))
        both = jnp.concatenate(parts, axis=1).astype(BF16)
        R[:, :, :, pl.ds(j * WIDE, WIDE)] = both.reshape(NY, NZ, 2 * CAP, WIDE)

    PART = D // 4

    def r_part(yy, p):
        return R.at[yy, :, :, pl.ds(p * PART, PART)]

    def r_hops(p, plus):
        return 4 if (p == 0) == plus else 3

    r_slot = {}
    for plus in (True, False):
        for p in range(2):
            for s in range(1, r_hops(p, plus) + 1):
                r_slot[p, s, plus] = len(r_slot)
    r_live = {}

    def r_dest(p, s, plus):
        d = r_hops(p, plus) - s + 1
        return (y + (d if plus else NY - d)) % NY

    def r_send(p, s, plus):
        r_live[p, s, plus] = go(
            r_part(r_dest(p, s, plus), p),
            yrecv.at[r_slot[p, s, plus]],
            north if plus else south,
        )

    def r_step(p, s, plus):
        r_live[p, s, plus].wait_recv()
        dest = r_dest(p, s + 1, plus)
        ref = r_part(dest, p)
        total = ref[...].astype(F32) + yrecv[r_slot[p, s, plus]].astype(F32)
        ref[...] = total.astype(BF16)
        r_send(p, s + 1, plus)

    for p, plus in ((0, True), (1, False), (1, True), (0, False)):
        r_send(p, 1, plus)

    for n, xx in enumerate(x_order):
        for zz in range(2):
            weight_grad(block_of(xx, zz, c))

    def core_sum(n, zz):
        core_copies[2 * n + zz].wait_recv()
        i = block_of(x_order[n], zz, c)
        T[i] = (T[i].astype(F32) + crecv[2 * n + zz].astype(F32)).astype(BF16)

    def t_ref(xx, zz):
        return T.at[block_of(xx, zz, c)]

    core_sum(0, 0)
    xp1 = go(t_ref(x2, 0), xrecv.at[0], right)
    core_sum(0, 1)
    xm1 = go(t_ref(x2, 1), xrecv.at[1], left)
    core_sum(1, 1)
    xp2 = go(t_ref(x1, 1), xrecv.at[2], right)
    core_sum(2, 0)
    xm2 = go(t_ref(x3, 0), xrecv.at[3], left)
    core_sum(1, 0)
    core_sum(2, 1)
    core_sum(3, 0)
    core_sum(3, 1)

    for p, plus in ((0, True), (1, False), (1, True), (0, False)):
        r_step(p, 1, plus)

    xp1.wait_recv()
    i = block_of(x1, 0, c)
    T[i] = (T[i].astype(F32) + xrecv[0].astype(F32)).astype(BF16)
    xp3 = go(t_ref(x1, 0), xrecv.at[4], right)
    xm1.wait_recv()
    i = block_of(x3, 1, c)
    T[i] = (T[i].astype(F32) + xrecv[1].astype(F32)).astype(BF16)
    xm3 = go(t_ref(x3, 1), xrecv.at[5], left)

    for p, plus in ((0, True), (1, False), (1, True), (0, False)):
        r_step(p, 2, plus)

    for one in (xp2, xm2, xp3, xm3):
        one.wait_recv()
    i = block_of(x, 1 - zh, c)
    from_left = xrecv[4 - 2 * (1 - zh)].astype(F32)
    from_right = xrecv[3 + 2 * (1 - zh)].astype(F32)
    zhsend[...] = (T[i].astype(F32) + from_left + from_right).astype(BF16)
    zh_copy = go(zhsend, zhrecv, other_run)

    for p, plus in ((0, True), (1, False)):
        r_step(p, 3, plus)

    z_live = []
    for p in range(2):
        for plus in (True, False):
            r_live[p, r_hops(p, plus), plus].wait_recv()
        ref = r_part(y, p)
        total = ref[...].astype(F32)
        for plus in (True, False):
            total = total + yrecv[r_slot[p, r_hops(p, plus), plus]].astype(F32)
        ref[...] = total.astype(BF16)
        base = sems.take(NZ)
        for j in range(1, NZ):
            zs = (zl + j) % NZ
            one = pltpu.make_async_remote_copy(
                src_ref=R.at[y, zs, :, pl.ds(p * PART, PART)],
                dst_ref=zrecv.at[p, zl],
                send_sem=send_sem.at[base + zs],
                recv_sem=recv_sem.at[base + zl],
                device_id=at(zl=zs),
                device_id_type=MESH,
            )
            one.start()
            sent.append(one)
        z_live.append(base)

    i = block_of(x, zh, c)
    total = T[i].astype(F32)
    total = total + xrecv[4 - 2 * zh].astype(F32) + xrecv[3 + 2 * zh].astype(F32)
    zh_copy.wait_recv()
    total = total + zhrecv[...].astype(F32)
    out_gu[0] = total[:UNITS]
    out_gu[1] = total[UNITS : 2 * UNITS]
    out_dn[...] = total[2 * UNITS :]

    placed = jnp.concatenate([picker, jnp.zeros((n_tok - 2 * CAP, n_tok), F32)], axis=0).T
    lane = lax.broadcasted_iota(jnp.int32, (n_tok, 2 * CAP), 1)
    placed = placed[:, : 2 * CAP]
    low = jnp.where(lane < CAP, placed, 0.0).astype(BF16)
    high = jnp.where(lane >= CAP, placed, 0.0).astype(BF16)
    for p in range(2):
        total = R[y, zl, :, pl.ds(p * PART, PART)].astype(F32)
        for j in range(1, NZ):
            zs = (zl + j) % NZ
            pltpu.make_async_remote_copy(
                src_ref=zrecv.at[p, zs],
                dst_ref=zrecv.at[p, zs],
                send_sem=send_sem.at[z_live[p] + zs],
                recv_sem=recv_sem.at[z_live[p] + zs],
                device_id=at(zl=zs),
                device_id_type=MESH,
            ).wait_recv()
            total = total + zrecv[p, zs].astype(F32)
        rows = total.astype(BF16)
        for part, base in ((low, 0), (high, D // 2)):
            grad = jnp.dot(part, rows, preferred_element_type=F32)
            out_tok[:, pl.ds(base + p * PART, PART)] = grad.astype(BF16)

    for one in sent:
        one.wait_send()
    for zs in z_sent:

        @pl.when((zs <= zl) & (zl < NZ - 1))
        def _():
            z_copy(zs, True).wait_send()

        @pl.when((zs >= zl) & (zl > 0))
        def _():
            z_copy(zs, False).wait_send()


def on_device(tokens_in, out_grad, routes, router_probs, gate_up, down_proj):
    vmem = pl.BlockSpec(memory_space=pltpu.VMEM)
    anywhere = pl.BlockSpec(memory_space=pl.ANY)
    n_tok = tokens_in.shape[0]
    blocks = NY * NZ
    n_sems = 160
    return pl.pallas_call(
        kernel,
        out_shape=(
            jax.ShapeDtypeStruct(tokens_in.shape, BF16),
            jax.ShapeDtypeStruct(gate_up.shape, F32),
            jax.ShapeDtypeStruct(down_proj.shape, F32),
        ),
        in_specs=[anywhere, anywhere, vmem, vmem, anywhere, anywhere],
        out_specs=(vmem, vmem, vmem),
        scratch_shapes=[
            pltpu.VMEM((n_tok, D), BF16),
            pltpu.VMEM((n_tok, D), BF16),
            pltpu.VMEM((blocks, 2 * CAP, D), BF16),
            pltpu.VMEM((3 * UNITS, D), BF16),
            pltpu.VMEM((3 * UNITS, 2 * CAP * blocks), BF16),
            pltpu.VMEM((CAP * blocks, 2 * UNITS), BF16),
            pltpu.VMEM((NY, NZ, 2 * CAP, D // 2), BF16),
            pltpu.VMEM((14, NZ, 2 * CAP, D // 4), BF16),
            pltpu.VMEM((2, NZ, 2 * CAP, D // 4), BF16),
            pltpu.VMEM((16, 3 * UNITS, COLS), BF16),
            pltpu.VMEM((8, 3 * UNITS, COLS), BF16),
            pltpu.VMEM((6, 3 * UNITS, COLS), BF16),
            pltpu.VMEM((3 * UNITS, COLS), BF16),
            pltpu.VMEM((3 * UNITS, COLS), BF16),
            pltpu.SemaphoreType.DMA((5,)),
            pltpu.SemaphoreType.DMA((n_sems,)),
            pltpu.SemaphoreType.DMA((n_sems,)),
        ],
        compiler_params=pltpu.CompilerParams(
            collective_id=0, has_side_effects=True, vmem_limit_bytes=48 * 2**20
        ),
        cost_estimate=pl.CostEstimate(
            flops=6 * 10**9, bytes_accessed=4 * 2**20, transcendentals=2**15
        ),
        name="expert_backward",
    )(tokens_in, out_grad, routes, router_probs, gate_up, down_proj)


def solution(mesh):
    in_specs = (
        P(("dp", "expert"), None),
        P(("dp", "expert"), None),
        P(("dp", "expert"), None),
        P(("dp", "expert"), None),
        P(None, "expert", "dp"),
        P("expert", "dp"),
    )
    out_specs = (P(("dp", "expert"), None), P(None, "expert", "dp"), P("expert", "dp"))
    return jax.shard_map(
        on_device, mesh=mesh, in_specs=in_specs, out_specs=out_specs, check_vma=False
    )
```

time: 664 us -> 112 us (0.17)
  waiting for transfers between devices: 616 us -> 0 us
  Pallas kernels: 0 us -> 104 us
  matrix products: 17.8 us -> 0 us
  between operations: 14.2 us -> 0.66 us
  starting transfers between devices: 7.78 us -> 0 us
  local copies, waits for them, and re-layouts: 0.13 us -> 7.22 us
  other arithmetic: 6.71 us -> 0 us
    all_gather x4 -> x0, waiting for transfers between devices: 433 us -> none  [the longest x1 150 us: on_device(): lax.all_gather(send_grad, 'expert', axis=0, tiled=True)]
    reduce_scatter x2 -> x0, waiting for transfers between devices: 182 us -> none  [the longest x1 96.7 us: on_device(): lax.psum_scatter(pair_term.astype(jnp.bfloat16), 'dp', scatter_dimension=...]
    pallas_call x0 -> x1, Pallas kernels: none -> 104 us  [on_device(): pl.pallas_call(kernel, out_shape=(jax.ShapeDtypeStruct(tokens_in.shape, B...]
    dot_general x8 -> x0, matrix products: 17.8 us -> none  [the longest x1 3.07 us: on_device(): jnp.einsum('ru,rd->ud', hidden, dispatched_grad, preferred_element_type=j...]
    all_to_all x1 -> x0, starting transfers between devices: 7.54 us -> none  [on_device(): lax.all_to_all(partial_rows, 'expert', split_axis=0, concat_axis=0, tiled...]
    unnamed x6 -> x13, local copies, waits for them, and re-layouts: 0.02 us -> 7.22 us
  transfers between devices with their start and end apart: 7 -> 0, of which waited for: 6 -> 0; matrix products, arithmetic and copies ran while one was open for 3% -> 0% of each run, Pallas kernels for 0% -> 0%
where the time goes in v1:
time: 112 us; the launch traced here: 111 us
  Pallas kernels  104 us (93%)
  local copies, waits for them, and re-layouts  7.22 us (6%)
    pallas_call x1, Pallas kernels, on_device(): pl.pallas_call(kernel, out_shape=(jax.ShapeDtypeStruct(tokens_in.shape, B...  104 us
    unnamed x13, local copies, waits for them, and re-layouts  7.22 us

profile of v1, /device:TPU:1, one launch (start us, length us, event | category | flops | bytes accessed | tf_op | source)
XLA Modules:
  0.0 111.4 jit_solution(18439565277504933356)
XLA Ops:
  0.6 0.0 copy-start.2
  0.6 0.8 copy.9.routes
  1.5 0.8 copy.10.probs
  2.2 0.0 copy-done.2
  2.2 0.0 copy-start
  2.3 1.2 %copy-done = bf16[128,4096]{1,0:T(8,128)(2,1)S(1)} copy-done((bf16[128,4096]{1,0:T(8,128)(2,1)S(1)}, bf16[128,4096]{1,0:T(8,128)(2,1)}, u32[]{:S(2)}) %copy-start) | copy-done | bytes 1048600
  3.5 0.0 copy-start.1
  3.5 1.2 %copy-done.1 = bf16[128,4096]{1,0:T(8,128)(2,1)S(1)} copy-done((bf16[128,4096]{1,0:T(8,128)(2,1)S(1)}, bf16[128,4096]{1,0:T(8,128)(2,1)}, u32[]{:S(2)}) %copy-start.1) | copy-done | bytes 1048600
  4.7 0.0 copy-start.3
  4.7 0.8 copy-done.3
  5.5 103.6 %expert_backward.1 = (bf16[128,4096]{1,0:T(8,128)(2,1)S(1)}, f32[2,128,256]{2,1,0:T(8,128)S(1)}, f32[128,256]{1,0:T(8,128)S(1)}) custom-call(bf16[128,4096]{1,0:T(8,128)(2,1)S(1)} %copy-done, bf16[128,4096]{1,0:T(8,128)(2,1)S(1)} %copy-done.1, s32[128,2]{1,0:T(8,128)S(1)} %copy.9.routes, f32[128,2]{1,0:T(8,128)S(1)} %copy.10.probs, ...), custom_call_target="tpu_custom_call" | custom-call | flops 6000000000 | bytes 4194304 | tf_op jit(solution)/shard_map/expert_backward/pallas_call | solution.py:421
  109.1 1.0 copy.14
  110.1 0.7 copy.15
  110.8 0.7 copy.16
Async XLA Ops:
  0.6 1.6 %copy-start.2 = (bf16[2,128,256]{2,1,0:T(8,128)(2,1)S(1)}, bf16[2,128,256]{2,1,0:T(8,128)(2,1)}, u32[]{:S(2)}) copy-start(bf16[2,128,256]{2,1,0:T(8,128)(2,1)} %gu_hbm.1) | copy-start | bytes 393220
  2.2 1.2 %copy-start = (bf16[128,4096]{1,0:T(8,128)(2,1)S(1)}, bf16[128,4096]{1,0:T(8,128)(2,1)}, u32[]{:S(2)}) copy-start(bf16[128,4096]{1,0:T(8,128)(2,1)} %tok_hbm.1) | copy-start | bytes 3145732
  3.5 1.2 %copy-start.1 = (bf16[128,4096]{1,0:T(8,128)(2,1)S(1)}, bf16[128,4096]{1,0:T(8,128)(2,1)}, u32[]{:S(2)}) copy-start(bf16[128,4096]{1,0:T(8,128)(2,1)} %og_hbm.1) | copy-start | bytes 3145732
  4.7 0.8 copy-start.3

commit v2 on v1

v2 whole, which is shorter than its diff:
```python
import jax
import jax.numpy as jnp
from jax import lax
from jax.experimental import pallas as pl
from jax.experimental.pallas import tpu as pltpu
from jax.sharding import PartitionSpec as P

MESH = pl.DeviceIdType.MESH
F32, BF16 = jnp.float32, jnp.bfloat16
NX, NY, NZ = 4, 8, 4
D = 4096
CAP = 8
COLS = 256
UNITS = 128
HALF = 3 * UNITS // 2
FIRST = 1408
PARTS = 4
PART = D // 2 // PARTS
CHUNKS = 3

AT_ENDS = (
    20000, 10011, 10010, 21000, 11011, 11010, 12011, 12010, 22000, 40000, 30000, 10021, 10020, 22100,
    20010, 10111, 10110, 11020, 12021, 12020, 22700, 11021, 21010, 11111, 11110, 50100, 50000, 10031,
    10030, 10121, 10120, 12031, 11031, 11030, 22200, 22600, 12030, 22010, 11121, 11120, 10130, 10131,
    10211, 10210, 11041, 12041, 20020, 22500, 10041, 11130, 21020, 22300, 10220, 60000, 11211, 11210,
    11140, 22710, 22110, 10221, 11221, 22400, 10230, 11220, 41000, 22210, 22610, 10140, 10231, 22020,
    11131, 10311, 20030, 10310, 11231, 10240, 22120, 22720, 11230, 22030, 11310, 11311, 22310, 21030,
    10321, 51100, 51000, 10320, 11321, 11320, 10331, 22510, 10330, 11331, 11240, 22220, 61000, 22730,
    22620, 11330, 10341, 11341, 22520, 22230, 22420, 22530, 22130, 22320, 22630, 22430, 22330, 22410,
)
INSIDE = (
    20000, 40000, 10011, 10010, 12010, 21000, 11011, 11010, 12011, 22000, 30000, 10021, 10020, 20010,
    10110, 20020, 10211, 10210, 11021, 10111, 11020, 12021, 12020, 22100, 22700, 21010, 11111, 11110,
    21020, 10031, 11211, 11210, 10030, 50000, 50100, 22010, 22020, 10121, 10120, 10221, 10220, 22600,
    60000, 12031, 11031, 12030, 22200, 22110, 22710, 11121, 10041, 20030, 10311, 10310, 11221, 11030,
    10130, 22720, 11220, 10131, 21030, 11311, 22210, 11310, 22120, 11120, 22030, 10230, 22610, 10231,
    12041, 22300, 22500, 11230, 10320, 22510, 22310, 11131, 22130, 22220, 10321, 22620, 11231, 10140,
    22730, 41000, 22630, 11320, 11321, 11130, 22410, 11041, 22330, 22530, 22320, 11140, 22400, 11240,
    22430, 22520, 11330, 51100, 10240, 10330, 10331, 22230, 51000, 11331, 10341, 22420, 61000, 11341,
)


def slots(routes, probs):
    n_tok = routes.shape[1]
    chosen = routes[...] == 0
    weight = jnp.sum(jnp.where(chosen, probs[...], 0.0), axis=0, keepdims=True)
    member = jnp.sum(jnp.where(chosen, 1.0, 0.0), axis=0, keepdims=True)
    weight = jnp.broadcast_to(weight, (2 * CAP, n_tok))
    member = jnp.broadcast_to(member, (2 * CAP, n_tok))
    before = lax.broadcasted_iota(jnp.int32, (n_tok, n_tok), 0)
    upto = lax.broadcasted_iota(jnp.int32, (n_tok, n_tok), 1)
    prefix = jnp.where(before <= upto, 1.0, 0.0).astype(BF16)
    position = jnp.dot(member.astype(BF16), prefix, preferred_element_type=F32)
    slot = (lax.broadcasted_iota(jnp.int32, (2 * CAP, n_tok), 0) % CAP).astype(F32)
    picker = jnp.where((position - 1.0 == slot) & (member > 0.5), 1.0, 0.0)
    return picker, jnp.sum(picker * weight, axis=1, keepdims=True)


class Sems:
    def __init__(self, send, recv):
        self.send, self.recv, self.used = send, recv, 0

    def take(self, n=1):
        at = self.used
        self.used += n
        return at


def kernel(
    tok_hbm, og_hbm, routes, probs, gu_hbm, dn_hbm,
    out_rows, out_w,
    tok, og, G, W, A_t, dH, R, yrecv, zrecv, T, crecv, xrecv, zhrecv, zhsend,
    load_sem, send_sem, recv_sem,
):
    dp, ex = lax.axis_index("dp"), lax.axis_index("expert")
    x, zh, c = dp // 4, (dp // 2) % 2, dp % 2
    zl, y = ex // NY, ex % NY

    def at(x=x, zh=zh, c=c, zl=zl, y=y):
        return ((x * 2 + zh) * 2 + c, zl * NY + y)

    right, left = at(x=(x + 1) % NX), at(x=(x + NX - 1) % NX)
    north, south = at(y=(y + 1) % NY), at(y=(y + NY - 1) % NY)
    other_core, other_run = at(c=1 - c), at(zh=1 - zh)
    in_run = [at(zl=(zl + j) % NZ) for j in range(1, NZ)]

    barrier = pltpu.get_barrier_semaphore()
    peers = [right, left, north, south, other_core, other_run] + in_run
    for peer in peers:
        pl.semaphore_signal(barrier, inc=1, device_id=peer, device_id_type=MESH)

    def cols(i):
        return pl.ds(pl.multiple_of(i * COLS, COLS), COLS)

    mine = cols(dp)
    loads = [
        pltpu.make_async_copy(tok_hbm, tok, load_sem.at[0]),
        pltpu.make_async_copy(og_hbm, og, load_sem.at[1]),
        pltpu.make_async_copy(gu_hbm.at[0], W.at[pl.ds(0, UNITS), mine], load_sem.at[2]),
        pltpu.make_async_copy(gu_hbm.at[1], W.at[pl.ds(UNITS, UNITS), mine], load_sem.at[3]),
        pltpu.make_async_copy(dn_hbm, W.at[pl.ds(2 * UNITS, UNITS), mine], load_sem.at[4]),
    ]
    for load in loads:
        load.start()

    picker, slot_weight = slots(routes, probs)
    picker_b = picker.astype(BF16)
    own_block = y * NZ + zl
    for load in loads:
        load.wait()
    x_rows = jnp.dot(picker_b, tok[...], preferred_element_type=F32)
    g_rows = jnp.dot(picker_b, og[...], preferred_element_type=F32)
    e_rows = slot_weight * g_rows
    G[own_block] = jnp.concatenate([x_rows[:CAP], e_rows[CAP:]], axis=0).astype(BF16)

    pl.semaphore_wait(barrier, len(peers))

    sems = Sems(send_sem, recv_sem)
    sent = []

    def copy(src, dst, device, k):
        return pltpu.make_async_remote_copy(
            src_ref=src,
            dst_ref=dst,
            send_sem=send_sem.at[k],
            recv_sem=recv_sem.at[k],
            device_id=device,
            device_id_type=MESH,
        )

    def go(src, dst, device, k=None):
        one = copy(src, dst, device, sems.take() if k is None else k)
        one.start()
        sent.append(one)
        return one

    upper = zl // 2
    m = zl * (1 - upper) + (3 - zl) * upper
    order = [b * (1 - upper) + (3 - b) * upper for b in (m, 1 - m, 2, 3)]

    col_parts = [pl.ds(0, FIRST), pl.ds(FIRST, FIRST), pl.ds(2 * FIRST, D - 2 * FIRST)]
    held = {}

    def sem_of(key, n=1):
        if key not in held:
            held[key] = sems.take(n)
        return held[key]

    def z_copy(part, d, zs, up):
        ref = G.at[(y + d) % NY * NZ + zs, :, col_parts[part]]
        to_send = sem_of(("up" if up else "down", part, d), NZ)
        return pltpu.make_async_remote_copy(
            src_ref=ref,
            dst_ref=ref,
            send_sem=send_sem.at[to_send + zs],
            recv_sem=recv_sem.at[sem_of(("up", part, d), NZ) + zs],
            device_id=at(zl=(zl + (1 if up else NZ - 1)) % NZ),
            device_id_type=MESH,
        )

    def z_both(act, part, d, zs):
        @pl.when((zs <= zl) & (zl < NZ - 1))
        def _():
            act(z_copy(part, d, zs, True))

        @pl.when((zs >= zl) & (zl > 0))
        def _():
            act(z_copy(part, d, zs, False))

    def start(one):
        one.start()

    def hops(k, plus):
        return 4 if (k in (0, 3)) == plus else 3

    def y_copy(part, k, h, plus):
        src_y = (y + (NY - h + 1 if plus else h - 1)) % NY
        ref = G.at[src_y * NZ + order[k], :, col_parts[part]]
        return copy(ref, ref, north if plus else south, sem_of(("y", part, k, h, plus)))

    def block_of(xx, zz, cc):
        return (xx * 2 + zz) * 2 + cc

    def w_ref(xx, zz, rows=pl.ds(0, 3 * UNITS), cc=c):
        return W.at[rows, cols(block_of(xx, zz, cc))]

    lo, hi = pl.ds(0, HALF), pl.ds(HALF, HALF)
    x1, x2, x3 = (x + 1) % NX, (x + 2) % NX, (x + 3) % NX
    runs = (zh, 1 - zh)

    def to_core(n, xx):
        ref = w_ref(xx, runs[n])
        return copy(ref, ref, other_core, sem_of(("core", n, [xx is one for one in (x, x1, x2, x3)].index(True))))

    def to_run():
        return copy(w_ref(x, zh), w_ref(x, zh), other_run, sem_of("run"))

    def x_copy(n, hop, plus):
        if hop == 1:
            ref = w_ref(x, runs[n])
        else:
            ref = w_ref(x3, runs[n], lo) if plus else w_ref(x1, runs[n], hi)
        return copy(ref, ref, right if plus else left, sem_of(("x", n, hop, plus)))

    y_keys = [(p, k, h, plus) for p in range(3) for k in range(4 if p < 2 else 1) for plus in (True, False) for h in range(1, hops(k, plus) + 1)]
    z_keys = [(p, d, k) for p in range(3) for d in range(1 if p < 2 else NY) for k in range(4)]
    x_keys = [(n, hop, plus) for n in range(2) for hop in (1, 2) for plus in (True, False)]
    core_keys = [(n, xx) for n in range(2) for xx in (x, x1, x2, x3)]

    def exchange(codes):
        taken = set()

        def take(one, *key):
            if key not in taken:
                taken.add(key)
                one().wait_recv()

        def take_y(*key):
            take(lambda: y_copy(*key), "y", *key)

        def take_z(p, d, k):
            take(lambda: z_copy(p, d, order[k], True), "z", p, d, k)

        for code in codes:
            kind, p, q, r, w = (code // 10**e % 10 for e in (4, 3, 2, 1, 0))
            if kind == 1:
                if r > 1:
                    take_y(p, q, r - 1, w == 1)
                elif q > 0:
                    take_z(p, 0, q)
                y_copy(p, q, r, w == 1).start()
            elif kind == 2:
                if r > 0:
                    take_z(p, q, r)
                elif q > 0:
                    take_y(p, 0, min(q, NY - q), q >= 4)
                z_both(start, p, q, order[r])
            elif kind == 3:
                to_run().start()
            elif kind == 4:
                if p == 1:
                    to_run().wait_recv()
                x_copy(p, 1, True).start()
                x_copy(p, 1, False).start()
                to_core(p, x).start()
            elif kind == 5:
                x_copy(p, 1, q == 1).wait_recv()
                x_copy(p, 2, q == 1).start()
                to_core(p, x3 if q == 1 else x1).start()
            else:
                x_copy(p, 2, True).wait_recv()
                x_copy(p, 2, False).wait_recv()
                to_core(p, x2).start()
        for key in y_keys:
            take_y(*key)
        for key in core_keys:
            to_core(*key).wait_recv()

    for key in y_keys:
        sem_of(("y", *key))

    @pl.when((zl == 0) | (zl == NZ - 1))
    def _():
        exchange(AT_ENDS)

    @pl.when((zl > 0) & (zl < NZ - 1))
    def _():
        exchange(INSIDE)

    for half in range(2):
        g = G[pl.ds(half * 16, 16)].reshape(256, D)
        pre = lax.dot_general(g, W[...], (((1,), (1,)), ((), ())), preferred_element_type=F32)
        pre = pre.reshape(16, 2 * CAP, 3 * UNITS)
        gate_pre = pre[:, :CAP, :UNITS]
        up_pre = pre[:, :CAP, UNITS : 2 * UNITS]
        hidden_grad = pre[:, CAP:, 2 * UNITS :]
        sig = 1.0 / (1.0 + jnp.exp(-gate_pre))
        activated = gate_pre * sig
        hidden = activated * up_pre
        up_grad = hidden_grad * activated
        gate_grad = hidden_grad * up_pre * sig * (1.0 + gate_pre * (1.0 - sig))
        zero = jnp.zeros_like(hidden)
        a = jnp.concatenate(
            [
                jnp.concatenate([gate_grad, up_grad, zero], axis=2),
                jnp.concatenate([zero, zero, hidden], axis=2),
            ],
            axis=1,
        ).reshape(256, 3 * UNITS)
        A_t[:, pl.ds(half * 256, 256)] = a.T.astype(BF16)
        grads = jnp.concatenate([gate_grad, up_grad], axis=2).reshape(128, 2 * UNITS)
        dH[pl.ds(half * 128, 128)] = grads.astype(BF16)

    def weight_grad(i):
        g = G[:, :, cols(i)].reshape(512, COLS)
        T[i] = jnp.dot(A_t[...], g, preferred_element_type=F32).astype(BF16)

    x_order = [x2, x1, x3, x]
    core_copies = []
    for n, xx in enumerate(x_order):
        for zz in range(2):
            i = block_of(xx, zz, 1 - c)
            weight_grad(i)
            core_copies.append(go(T.at[i], crecv.at[2 * n + zz], other_core))

    def r_part(yy, p):
        return R.at[yy, :, :, pl.ds(p * PART, PART)]

    def r_hops(p, plus):
        return 4 if (p % 2 == 0) == plus else 3

    r_slot = {}
    for plus in (True, False):
        for p in range(PARTS):
            for s in range(1, r_hops(p, plus) + 1):
                r_slot[p, s, plus] = len(r_slot)
    r_live = {}

    def r_dest(p, s, plus):
        d = r_hops(p, plus) - s + 1
        return (y + (d if plus else NY - d)) % NY

    def r_send(p, s, plus):
        r_live[p, s, plus] = go(
            r_part(r_dest(p, s, plus), p),
            yrecv.at[r_slot[p, s, plus]],
            north if plus else south,
        )

    def r_step(p, s, plus):
        r_live[p, s, plus].wait_recv()
        dest = r_dest(p, s + 1, plus)
        ref = r_part(dest, p)
        total = ref[...].astype(F32) + yrecv[r_slot[p, s, plus]].astype(F32)
        ref[...] = total.astype(BF16)
        r_send(p, s + 1, plus)

    def r_steps(s, parts):
        for p in parts:
            for plus in (True, False):
                if s < r_hops(p, plus):
                    r_step(p, s, plus)

    for p in range(PARTS):
        parts = []
        for base in (0, D // 2):
            w = W[pl.ds(0, 2 * UNITS), pl.ds(base + p * PART, PART)]
            part = jnp.dot(dH[...], w, preferred_element_type=F32)
            parts.append(part.reshape(NY * NZ, CAP, PART))
        both = jnp.concatenate(parts, axis=1).astype(BF16)
        R[:, :, :, pl.ds(p * PART, PART)] = both.reshape(NY, NZ, 2 * CAP, PART)
        for plus in (True, False):
            r_send(p, 1, plus)

    for n, xx in enumerate(x_order):
        for zz in range(2):
            weight_grad(block_of(xx, zz, c))

    def core_sum(n, zz):
        core_copies[2 * n + zz].wait_recv()
        i = block_of(x_order[n], zz, c)
        T[i] = (T[i].astype(F32) + crecv[2 * n + zz].astype(F32)).astype(BF16)

    CH = 3 * UNITS // CHUNKS

    def t_ref(xx, zz, q):
        return T.at[block_of(xx, zz, c), pl.ds(q * CH, CH)]

    def x_ref(slot, q):
        return xrecv.at[slot, pl.ds(q * CH, CH)]

    chunks = range(CHUNKS)
    xp1, xm1, xp2, xm2, xp3, xm3 = {}, {}, {}, {}, {}, {}
    core_sum(0, 0)
    core_sum(0, 1)
    for q in chunks:
        xp1[q] = go(t_ref(x2, 0, q), x_ref(0, q), right)
        xm1[q] = go(t_ref(x2, 1, q), x_ref(1, q), left)
    core_sum(1, 1)
    core_sum(2, 0)
    for q in chunks:
        xp2[q] = go(t_ref(x1, 1, q), x_ref(2, q), right)
        xm2[q] = go(t_ref(x3, 0, q), x_ref(3, q), left)
    core_sum(1, 0)
    core_sum(2, 1)
    core_sum(3, 0)
    core_sum(3, 1)

    def x_turn(q):
        for live, slot, xx, zz in ((xp1, 0, x1, 0), (xm1, 1, x3, 1)):
            live[q].wait_recv()
            ref = t_ref(xx, zz, q)
            ref[...] = (ref[...].astype(F32) + x_ref(slot, q)[...].astype(F32)).astype(BF16)
        xp3[q] = go(t_ref(x1, 0, q), x_ref(4, q), right)
        xm3[q] = go(t_ref(x3, 1, q), x_ref(5, q), left)

    zh_copy = {}

    def x_end(q):
        for live in (xp2, xm2, xp3, xm3):
            live[q].wait_recv()
        rows = pl.ds(q * CH, CH)
        total = t_ref(x, 1 - zh, q)[...].astype(F32)
        total = total + xrecv[4 - 2 * (1 - zh), rows].astype(F32)
        total = total + xrecv[3 + 2 * (1 - zh), rows].astype(F32)
        zhsend[rows] = total.astype(BF16)
        zh_copy[q] = go(zhsend.at[rows], zhrecv.at[rows], other_run)

    z_live = {}

    def r_end(p):
        for plus in (True, False):
            r_live[p, r_hops(p, plus), plus].wait_recv()
        ref = r_part(y, p)
        total = ref[...].astype(F32)
        for plus in (True, False):
            total = total + yrecv[r_slot[p, r_hops(p, plus), plus]].astype(F32)
        ref[...] = total.astype(BF16)
        base = sems.take(NZ)
        for j in range(1, NZ):
            zs = (zl + j) % NZ
            one = pltpu.make_async_remote_copy(
                src_ref=R.at[y, zs, :, pl.ds(p * PART, PART)],
                dst_ref=zrecv.at[p, zl],
                send_sem=send_sem.at[base + zs],
                recv_sem=recv_sem.at[base + zl],
                device_id=at(zl=zs),
                device_id_type=MESH,
            )
            one.start()
            sent.append(one)
        z_live[p] = base

    all_parts = range(PARTS)
    r_steps(1, all_parts)
    for q in chunks:
        x_turn(q)
    r_steps(2, all_parts)
    for q in chunks:
        x_end(q)
    r_steps(3, all_parts)
    for p in all_parts:
        r_end(p)

    for q in chunks:
        rows = pl.ds(q * CH, CH)
        total = t_ref(x, zh, q)[...].astype(F32)
        total = total + xrecv[4 - 2 * zh, rows].astype(F32) + xrecv[3 + 2 * zh, rows].astype(F32)
        zh_copy[q].wait_recv()
        out_w[rows] = total + zhrecv[rows].astype(F32)

    for p in all_parts:
        total = R[y, zl, :, pl.ds(p * PART, PART)].astype(F32)
        for j in range(1, NZ):
            zs = (zl + j) % NZ
            pltpu.make_async_remote_copy(
                src_ref=zrecv.at[p, zs],
                dst_ref=zrecv.at[p, zs],
                send_sem=send_sem.at[z_live[p] + zs],
                recv_sem=recv_sem.at[z_live[p] + zs],
                device_id=at(zl=zs),
                device_id_type=MESH,
            ).wait_recv()
            total = total + zrecv[p, zs].astype(F32)
        out_rows[:, pl.ds(p * PART, PART)] = total.astype(BF16)

    for one in sent:
        one.wait_send()
    for key in y_keys:
        y_copy(*key).wait_send()
    for p, d, k in z_keys:
        z_both(lambda one: one.wait_send(), p, d, order[k])
    for key in x_keys:
        x_copy(*key).wait_send()
    for key in core_keys:
        to_core(*key).wait_send()
    to_run().wait_send()


def finish(routes, probs, rows_hbm, grads_hbm, out_tok, out_gu, out_dn, rows, grads, buf, sem):
    copies = [
        pltpu.make_async_copy(grads.at[pl.ds(0, UNITS)], out_gu.at[0], sem.at[0]),
        pltpu.make_async_copy(grads.at[pl.ds(UNITS, UNITS)], out_gu.at[1], sem.at[1]),
        pltpu.make_async_copy(grads.at[pl.ds(2 * UNITS, UNITS)], out_dn, sem.at[2]),
    ]
    loads = [
        pltpu.make_async_copy(rows_hbm, rows, sem.at[5]),
        pltpu.make_async_copy(grads_hbm, grads, sem.at[6]),
    ]
    for load in loads:
        load.start()
    n_tok = out_tok.shape[0]
    picker, _ = slots(routes, probs)
    placed = jnp.concatenate([picker, jnp.zeros((n_tok - 2 * CAP, n_tok), F32)], axis=0).T
    placed = placed[:, : 2 * CAP]
    lane = lax.broadcasted_iota(jnp.int32, (n_tok, 2 * CAP), 1)
    low = jnp.where(lane < CAP, placed, 0.0).astype(BF16)
    high = jnp.where(lane >= CAP, placed, 0.0).astype(BF16)
    loads[1].wait()
    for one in copies:
        one.start()
    loads[0].wait()
    for n, part in enumerate((low, high)):
        at = pl.ds(n * (D // 2), D // 2)
        buf[:, at] = jnp.dot(part, rows[...], preferred_element_type=F32).astype(BF16)
        one = pltpu.make_async_copy(buf.at[:, at], out_tok.at[:, at], sem.at[3 + n])
        one.start()
        copies.append(one)
    for one in copies:
        one.wait()


def on_device(tokens_in, out_grad, routes, router_probs, gate_up, down_proj):
    vmem = pl.BlockSpec(memory_space=pltpu.VMEM)
    hbm = pl.BlockSpec(memory_space=pltpu.HBM)
    n_tok = tokens_in.shape[0]
    blocks = NY * NZ
    n_sems = 320
    routes, router_probs = routes.T, router_probs.T
    rows, grads = pl.pallas_call(
        kernel,
        out_shape=(
            jax.ShapeDtypeStruct((2 * CAP, D // 2), BF16),
            jax.ShapeDtypeStruct((3 * UNITS, COLS), F32),
        ),
        in_specs=[hbm, hbm, vmem, vmem, hbm, hbm],
        out_specs=(vmem, vmem),
        scratch_shapes=[
            pltpu.VMEM((n_tok, D), BF16),
            pltpu.VMEM((n_tok, D), BF16),
            pltpu.VMEM((blocks, 2 * CAP, D), BF16),
            pltpu.VMEM((3 * UNITS, D), BF16),
            pltpu.VMEM((3 * UNITS, 2 * CAP * blocks), BF16),
            pltpu.VMEM((CAP * blocks, 2 * UNITS), BF16),
            pltpu.VMEM((NY, NZ, 2 * CAP, D // 2), BF16),
            pltpu.VMEM((7 * PARTS, NZ, 2 * CAP, PART), BF16),
            pltpu.VMEM((PARTS, NZ, 2 * CAP, PART), BF16),
            pltpu.VMEM((16, 3 * UNITS, COLS), BF16),
            pltpu.VMEM((8, 3 * UNITS, COLS), BF16),
            pltpu.VMEM((6, 3 * UNITS, COLS), BF16),
            pltpu.VMEM((3 * UNITS, COLS), BF16),
            pltpu.VMEM((3 * UNITS, COLS), BF16),
            pltpu.SemaphoreType.DMA((5,)),
            pltpu.SemaphoreType.DMA((n_sems,)),
            pltpu.SemaphoreType.DMA((n_sems,)),
        ],
        compiler_params=pltpu.CompilerParams(
            collective_id=0, has_side_effects=True, vmem_limit_bytes=56 * 2**20
        ),
        cost_estimate=pl.CostEstimate(
            flops=6 * 10**9, bytes_accessed=4 * 2**20, transcendentals=2**15
        ),
        name="expert_backward",
    )(tokens_in, out_grad, routes, router_probs, gate_up, down_proj)
    return pl.pallas_call(
        finish,
        out_shape=(
            jax.ShapeDtypeStruct(tokens_in.shape, BF16),
            jax.ShapeDtypeStruct(gate_up.shape, F32),
            jax.ShapeDtypeStruct(down_proj.shape, F32),
        ),
        in_specs=[vmem, vmem, hbm, hbm],
        out_specs=(hbm, hbm, hbm),
        scratch_shapes=[
            pltpu.VMEM((2 * CAP, D // 2), BF16),
            pltpu.VMEM((3 * UNITS, COLS), F32),
            pltpu.VMEM((n_tok, D), BF16),
            pltpu.SemaphoreType.DMA((7,)),
        ],
        name="finish",
    )(routes, router_probs, rows, grads)


def solution(mesh):
    in_specs = (
        P(("dp", "expert"), None),
        P(("dp", "expert"), None),
        P(("dp", "expert"), None),
        P(("dp", "expert"), None),
        P(None, "expert", "dp"),
        P("expert", "dp"),
    )
    out_specs = (P(("dp", "expert"), None), P(None, "expert", "dp"), P("expert", "dp"))
    return jax.shard_map(
        on_device, mesh=mesh, in_specs=in_specs, out_specs=out_specs, check_vma=False
    )
```

time: 112 us -> 95.6 us (0.85)
  Pallas kernels: 104 us -> 94.1 us
  local copies, waits for them, and re-layouts: 7.22 us -> 0 us
    pallas_call x1 -> x2, Pallas kernels: 104 us -> 94.1 us  [the longest x1 91 us: on_device(): pl.pallas_call(kernel, out_shape=(jax.ShapeDtypeStruct((2 * CAP, D // 2),...]
    unnamed x13 -> x0, local copies, waits for them, and re-layouts: 7.22 us -> none
where the time goes in v2:
time: 95.6 us; the launch traced here: 94.7 us
  Pallas kernels  94.1 us (98%)
    pallas_call x1, Pallas kernels, on_device(): pl.pallas_call(kernel, out_shape=(jax.ShapeDtypeStruct((2 * CAP, D // 2),...  91 us
    pallas_call x1, Pallas kernels, on_device(): pl.pallas_call(finish, out_shape=(jax.ShapeDtypeStruct(tokens_in.shape, B...  3.04 us

profile of v2, /device:TPU:1, one launch (start us, length us, event | category | flops | bytes accessed | tf_op | source)
XLA Modules:
  0.0 94.7 jit_solution(11453748547121110430)
XLA Ops:
  0.6 91.0 %expert_backward.1 = (bf16[16,2048]{1,0:T(8,128)(2,1)}, f32[384,256]{1,0:T(8,128)}) custom-call(bf16[128,4096]{1,0:T(8,128)(2,1)} %tok_hbm.1, bf16[128,4096]{1,0:T(8,128)(2,1)} %og_hbm.1, s32[2,128]{1,0:T(2,128)} %bitcast.2, f32[2,128]{1,0:T(2,128)} %bitcast.4, bf16[2,128,256]{2,1,0:T(8,128)(2,1)} %gu_hbm.1, bf16[128,256]{1,0:T(8,128)(2,1)} %dn_hbm.1), custom_call_target="tpu_custom_call" | custom-call | flops 6000000000 | bytes 4194304 | tf_op jit(solution)/shard_map/expert_backward/pallas_call | solution.py:520
  91.7 3.0 %finish.1 = (bf16[128,4096]{1,0:T(8,128)(2,1)}, f32[2,128,256]{2,1,0:T(8,128)}, f32[128,256]{1,0:T(8,128)}) custom-call(s32[2,128]{1,0:T(2,128)} %bitcast.3, f32[2,128]{1,0:T(2,128)} %bitcast.5, bf16[16,2048]{1,0:T(8,128)(2,1)} %get-tuple-element.5.rows_hbm, f32[384,256]{1,0:T(8,128)} %get-tuple-element.6.grads_hbm), custom_call_target="tpu_custom_call" | custom-call | tf_op jit(solution)/shard_map/finish/pallas_call | solution.py:555

commit v3 on v2

--- a/solution.py
+++ b/solution.py
@@ -16,27 +16,39 @@
 FIRST = 1408
 PARTS = 4
 PART = D // 2 // PARTS
-CHUNKS = 3
-
+CHUNKS = 2
+X_ROWS = 256
+CH = X_ROWS // CHUNKS
+Z_ROWS = 3 * UNITS - X_ROWS
+
+AFTER = (
+    10010, 11000, 10000, 12100, 11100, 10100, 12010, 10110, 11200, 12310, 12300, 12110, 12000, 10210,
+    10200, 13010, 14100, 13000, 22000, 14010, 11300, 14110, 14000, 12210, 13110, 10310, 13100, 22100,
+    19010, 10300, 19011, 12200, 13200, 13210, 15010, 22200, 15100, 19110, 19111, 19211, 15110, 19210,
+    16000, 16010, 15000, 19310, 19021, 19311, 16100, 13310, 19020, 16110, 13300, 22300, 23000, 19120,
+    19221, 19121, 24000, 24100, 19220, 17000, 19320, 17100, 23100, 19031, 19130, 26100, 19321, 23200,
+    25100, 26000, 19231, 19330, 20000, 25000, 20100, 20200, 23300, 20300, 21100, 18100, 18000, 27000,
+    21000, 21200, 21300,
+)
 AT_ENDS = (
-    20000, 10011, 10010, 21000, 11011, 11010, 12011, 12010, 22000, 40000, 30000, 10021, 10020, 22100,
-    20010, 10111, 10110, 11020, 12021, 12020, 22700, 11021, 21010, 11111, 11110, 50100, 50000, 10031,
-    10030, 10121, 10120, 12031, 11031, 11030, 22200, 22600, 12030, 22010, 11121, 11120, 10130, 10131,
-    10211, 10210, 11041, 12041, 20020, 22500, 10041, 11130, 21020, 22300, 10220, 60000, 11211, 11210,
-    11140, 22710, 22110, 10221, 11221, 22400, 10230, 11220, 41000, 22210, 22610, 10140, 10231, 22020,
-    11131, 10311, 20030, 10310, 11231, 10240, 22120, 22720, 11230, 22030, 11310, 11311, 22310, 21030,
-    10321, 51100, 51000, 10320, 11321, 11320, 10331, 22510, 10330, 11331, 11240, 22220, 61000, 22730,
-    22620, 11330, 10341, 11341, 22520, 22230, 22420, 22530, 22130, 22320, 22630, 22430, 22330, 22410,
+    11010, 21000, 11011, 20000, 12010, 10011, 10010, 12011, 40000, 30000, 11111, 11110, 11021, 11020,
+    22100, 10111, 10110, 12021, 12020, 10021, 10020, 22000, 21010, 11121, 11120, 20010, 50000, 11031,
+    11030, 10121, 50100, 22600, 22200, 10120, 12031, 12030, 10031, 22700, 10030, 11130, 21020, 11211,
+    11210, 22110, 11041, 20020, 10211, 11131, 10210, 60000, 22010, 41000, 10130, 22500, 12041, 10041,
+    11140, 10131, 22300, 11220, 10220, 11221, 10140, 22710, 11311, 22210, 11310, 22400, 11230, 10311,
+    20030, 10221, 21030, 10310, 22020, 22120, 22720, 22610, 22220, 11231, 11321, 10230, 10321, 51100,
+    11320, 11240, 51000, 10231, 10240, 10320, 11331, 22310, 22030, 22620, 10331, 61000, 11330, 11341,
+    22530, 22510, 22130, 10341, 10330, 22430, 22630, 22320, 22420, 22730, 22230, 22330, 22410, 22520,
 )
 INSIDE = (
-    20000, 40000, 10011, 10010, 12010, 21000, 11011, 11010, 12011, 22000, 30000, 10021, 10020, 20010,
-    10110, 20020, 10211, 10210, 11021, 10111, 11020, 12021, 12020, 22100, 22700, 21010, 11111, 11110,
-    21020, 10031, 11211, 11210, 10030, 50000, 50100, 22010, 22020, 10121, 10120, 10221, 10220, 22600,
-    60000, 12031, 11031, 12030, 22200, 22110, 22710, 11121, 10041, 20030, 10311, 10310, 11221, 11030,
-    10130, 22720, 11220, 10131, 21030, 11311, 22210, 11310, 22120, 11120, 22030, 10230, 22610, 10231,
-    12041, 22300, 22500, 11230, 10320, 22510, 22310, 11131, 22130, 22220, 10321, 22620, 11231, 10140,
-    22730, 41000, 22630, 11320, 11321, 11130, 22410, 11041, 22330, 22530, 22320, 11140, 22400, 11240,
-    22430, 22520, 11330, 51100, 10240, 10330, 10331, 22230, 51000, 11331, 10341, 22420, 61000, 11341,
+    21000, 11011, 11010, 20000, 12011, 12010, 10011, 10010, 40000, 11210, 11021, 30000, 21020, 21010,
+    11211, 11111, 20010, 20020, 11110, 10021, 11020, 10211, 10111, 10110, 10210, 22100, 22000, 22700,
+    11220, 12020, 50100, 50000, 12021, 11221, 11120, 11031, 11121, 11030, 12031, 22200, 21030, 10020,
+    10221, 10120, 11311, 22600, 11310, 10220, 10311, 22020, 10031, 10121, 60000, 10310, 11231, 11130,
+    22110, 20030, 22710, 11131, 22610, 22220, 12030, 22720, 22010, 11041, 22120, 10030, 22310, 11230,
+    22620, 11320, 10231, 22210, 11321, 22510, 41000, 12041, 22500, 10131, 22130, 10041, 22300, 10230,
+    10320, 22030, 22730, 11140, 10321, 22410, 22530, 10130, 22320, 51000, 22230, 11330, 10330, 11240,
+    51100, 11331, 22520, 22330, 10140, 22400, 10331, 22630, 10240, 11341, 22430, 61000, 10341, 22420,
 )
 
 
@@ -67,9 +79,9 @@
 
 
 def kernel(
-    tok_hbm, og_hbm, routes, probs, gu_hbm, dn_hbm,
-    out_rows, out_w,
-    tok, og, G, W, A_t, dH, R, yrecv, zrecv, T, crecv, xrecv, zhrecv, zhsend,
+    tok_hbm, og_hbm, routes_hbm, probs_hbm, gu_hbm, dn_hbm,
+    rows_hbm, w_hbm,
+    routes, probs, out_rows, out_w, tok, og, G, W, A_t, dH, R, yrecv, zrecv, T, crecv, xrecv, zhrecv, zhsend, zwrecv, hrecv,
     load_sem, send_sem, recv_sem,
 ):
     dp, ex = lax.axis_index("dp"), lax.axis_index("expert")
@@ -93,6 +105,10 @@
         return pl.ds(pl.multiple_of(i * COLS, COLS), COLS)
 
     mine = cols(dp)
+    routing = [
+        pltpu.make_async_copy(routes_hbm, routes, load_sem.at[5]),
+        pltpu.make_async_copy(probs_hbm, probs, load_sem.at[6]),
+    ]
     loads = [
         pltpu.make_async_copy(tok_hbm, tok, load_sem.at[0]),
         pltpu.make_async_copy(og_hbm, og, load_sem.at[1]),
@@ -100,8 +116,10 @@
         pltpu.make_async_copy(gu_hbm.at[1], W.at[pl.ds(UNITS, UNITS), mine], load_sem.at[3]),
         pltpu.make_async_copy(dn_hbm, W.at[pl.ds(2 * UNITS, UNITS), mine], load_sem.at[4]),
     ]
-    for load in loads:
+    for load in routing + loads:
         load.start()
+    for load in routing:
+        load.wait()
 
     picker, slot_weight = slots(routes, probs)
     picker_b = picker.astype(BF16)
@@ -295,13 +313,27 @@
         g = G[:, :, cols(i)].reshape(512, COLS)
         T[i] = jnp.dot(A_t[...], g, preferred_element_type=F32).astype(BF16)
 
+    written = []
     x_order = [x2, x1, x3, x]
-    core_copies = []
-    for n, xx in enumerate(x_order):
-        for zz in range(2):
-            i = block_of(xx, zz, 1 - c)
-            weight_grad(i)
-            core_copies.append(go(T.at[i], crecv.at[2 * n + zz], other_core))
+
+    def begin(one):
+        one.start()
+        sent.append(one)
+
+    def add(ref, *terms):
+        total = ref[...].astype(F32)
+        for term in terms:
+            total = total + term.astype(F32)
+        return total
+
+    def core_copy(n, zz):
+        i = block_of(x_order[n], zz, 1 - c)
+        return copy(T.at[i], crecv.at[2 * n + zz], other_core, sem_of(("c", n, zz)))
+
+    def core_sum(n, zz):
+        core_copy(n, zz).wait_recv()
+        ref = T.at[block_of(x_order[n], zz, c)]
+        ref[...] = add(ref, crecv[2 * n + zz]).astype(BF16)
 
     def r_part(yy, p):
         return R.at[yy, :, :, pl.ds(p * PART, PART)]
@@ -314,34 +346,22 @@
         for p in range(PARTS):
             for s in range(1, r_hops(p, plus) + 1):
                 r_slot[p, s, plus] = len(r_slot)
-    r_live = {}
 
     def r_dest(p, s, plus):
         d = r_hops(p, plus) - s + 1
         return (y + (d if plus else NY - d)) % NY
 
-    def r_send(p, s, plus):
-        r_live[p, s, plus] = go(
-            r_part(r_dest(p, s, plus), p),
-            yrecv.at[r_slot[p, s, plus]],
-            north if plus else south,
-        )
+    def r_copy(p, s, plus):
+        src, dst = r_part(r_dest(p, s, plus), p), yrecv.at[r_slot[p, s, plus]]
+        return copy(src, dst, north if plus else south, sem_of(("r", p, s, plus)))
 
     def r_step(p, s, plus):
-        r_live[p, s, plus].wait_recv()
-        dest = r_dest(p, s + 1, plus)
-        ref = r_part(dest, p)
-        total = ref[...].astype(F32) + yrecv[r_slot[p, s, plus]].astype(F32)
-        ref[...] = total.astype(BF16)
-        r_send(p, s + 1, plus)
-
-    def r_steps(s, parts):
-        for p in parts:
-            for plus in (True, False):
-                if s < r_hops(p, plus):
-                    r_step(p, s, plus)
-
-    for p in range(PARTS):
+        r_copy(p, s, plus).wait_recv()
+        ref = r_part(r_dest(p, s + 1, plus), p)
+        ref[...] = add(ref, yrecv[r_slot[p, s, plus]]).astype(BF16)
+        begin(r_copy(p, s + 1, plus))
+
+    def row_grad(p):
         parts = []
         for base in (0, D // 2):
             w = W[pl.ds(0, 2 * UNITS), pl.ds(base + p * PART, PART)]
@@ -350,120 +370,160 @@
         both = jnp.concatenate(parts, axis=1).astype(BF16)
         R[:, :, :, pl.ds(p * PART, PART)] = both.reshape(NY, NZ, 2 * CAP, PART)
         for plus in (True, False):
-            r_send(p, 1, plus)
-
-    for n, xx in enumerate(x_order):
-        for zz in range(2):
-            weight_grad(block_of(xx, zz, c))
-
-    def core_sum(n, zz):
-        core_copies[2 * n + zz].wait_recv()
-        i = block_of(x_order[n], zz, c)
-        T[i] = (T[i].astype(F32) + crecv[2 * n + zz].astype(F32)).astype(BF16)
-
-    CH = 3 * UNITS // CHUNKS
-
-    def t_ref(xx, zz, q):
-        return T.at[block_of(xx, zz, c), pl.ds(q * CH, CH)]
-
-    def x_ref(slot, q):
-        return xrecv.at[slot, pl.ds(q * CH, CH)]
-
-    chunks = range(CHUNKS)
-    xp1, xm1, xp2, xm2, xp3, xm3 = {}, {}, {}, {}, {}, {}
-    core_sum(0, 0)
-    core_sum(0, 1)
-    for q in chunks:
-        xp1[q] = go(t_ref(x2, 0, q), x_ref(0, q), right)
-        xm1[q] = go(t_ref(x2, 1, q), x_ref(1, q), left)
-    core_sum(1, 1)
-    core_sum(2, 0)
-    for q in chunks:
-        xp2[q] = go(t_ref(x1, 1, q), x_ref(2, q), right)
-        xm2[q] = go(t_ref(x3, 0, q), x_ref(3, q), left)
-    core_sum(1, 0)
-    core_sum(2, 1)
-    core_sum(3, 0)
-    core_sum(3, 1)
-
-    def x_turn(q):
-        for live, slot, xx, zz in ((xp1, 0, x1, 0), (xm1, 1, x3, 1)):
-            live[q].wait_recv()
-            ref = t_ref(xx, zz, q)
-            ref[...] = (ref[...].astype(F32) + x_ref(slot, q)[...].astype(F32)).astype(BF16)
-        xp3[q] = go(t_ref(x1, 0, q), x_ref(4, q), right)
-        xm3[q] = go(t_ref(x3, 1, q), x_ref(5, q), left)
-
-    zh_copy = {}
+            begin(r_copy(p, 1, plus))
+
+    def run_copy(p, zs, arriving):
+        base = sem_of(("run", p), NZ)
+        return pltpu.make_async_remote_copy(
+            src_ref=R.at[y, zs, :, pl.ds(p * PART, PART)],
+            dst_ref=zrecv.at[p, zs if arriving else zl],
+            send_sem=send_sem.at[base + zs],
+            recv_sem=recv_sem.at[base + (zs if arriving else zl)],
+            device_id=at(zl=zs),
+            device_id_type=MESH,
+        )
+
+    def r_end(p):
+        ways = (True, False)
+        for plus in ways:
+            r_copy(p, r_hops(p, plus), plus).wait_recv()
+        ref = r_part(y, p)
+        terms = [yrecv[r_slot[p, r_hops(p, plus), plus]] for plus in ways]
+        ref[...] = add(ref, *terms).astype(BF16)
+        for j in range(1, NZ):
+            begin(run_copy(p, (zl + j) % NZ, False))
+
+    def r_final(p):
+        others = [(zl + j) % NZ for j in range(1, NZ)]
+        for zs in others:
+            run_copy(p, zs, True).wait_recv()
+        here = pl.ds(p * PART, PART)
+        total = add(R.at[y, zl, :, here], *[zrecv[p, zs] for zs in others])
+        out_rows[:, here] = total.astype(BF16)
+
+    def t_ref(xx, zz, rows):
+        return T.at[block_of(xx, zz, c), rows]
+
+    def x_rows_of(q):
+        return pl.ds(q * CH, CH)
+
+    def t_copy(step, q, plus):
+        xx, zz = {
+            (1, True): (x2, 0), (1, False): (x2, 1), (2, True): (x1, 1),
+            (2, False): (x3, 0), (3, True): (x1, 0), (3, False): (x3, 1),
+        }[step, plus]
+        slot = 2 * (step - 1) + (0 if plus else 1)
+        src, dst = t_ref(xx, zz, x_rows_of(q)), xrecv.at[slot, x_rows_of(q)]
+        return copy(src, dst, right if plus else left, sem_of(("t", step, q, plus)))
+
+    def x_turn(q, plus):
+        t_copy(1, q, plus).wait_recv()
+        ref = t_ref(x1, 0, x_rows_of(q)) if plus else t_ref(x3, 1, x_rows_of(q))
+        ref[...] = add(ref, xrecv[0 if plus else 1, x_rows_of(q)]).astype(BF16)
+        begin(t_copy(3, q, plus))
+
+    def x_total(zz, rows):
+        return add(t_ref(x, zz, rows), xrecv[4 - 2 * zz, rows], xrecv[3 + 2 * zz, rows])
+
+    def zh_copy(q):
+        rows = x_rows_of(q)
+        return copy(zhsend.at[rows], zhrecv.at[rows], other_run, sem_of(("zh", q)))
 
     def x_end(q):
-        for live in (xp2, xm2, xp3, xm3):
-            live[q].wait_recv()
-        rows = pl.ds(q * CH, CH)
-        total = t_ref(x, 1 - zh, q)[...].astype(F32)
-        total = total + xrecv[4 - 2 * (1 - zh), rows].astype(F32)
-        total = total + xrecv[3 + 2 * (1 - zh), rows].astype(F32)
-        zhsend[rows] = total.astype(BF16)
-        zh_copy[q] = go(zhsend.at[rows], zhrecv.at[rows], other_run)
-
-    z_live = {}
-
-    def r_end(p):
-        for plus in (True, False):
-            r_live[p, r_hops(p, plus), plus].wait_recv()
-        ref = r_part(y, p)
-        total = ref[...].astype(F32)
-        for plus in (True, False):
-            total = total + yrecv[r_slot[p, r_hops(p, plus), plus]].astype(F32)
-        ref[...] = total.astype(BF16)
-        base = sems.take(NZ)
-        for j in range(1, NZ):
-            zs = (zl + j) % NZ
-            one = pltpu.make_async_remote_copy(
-                src_ref=R.at[y, zs, :, pl.ds(p * PART, PART)],
-                dst_ref=zrecv.at[p, zl],
-                send_sem=send_sem.at[base + zs],
-                recv_sem=recv_sem.at[base + zl],
-                device_id=at(zl=zs),
-                device_id_type=MESH,
-            )
-            one.start()
-            sent.append(one)
-        z_live[p] = base
-
-    all_parts = range(PARTS)
-    r_steps(1, all_parts)
-    for q in chunks:
-        x_turn(q)
-    r_steps(2, all_parts)
-    for q in chunks:
-        x_end(q)
-    r_steps(3, all_parts)
-    for p in all_parts:
-        r_end(p)
-
-    for q in chunks:
-        rows = pl.ds(q * CH, CH)
-        total = t_ref(x, zh, q)[...].astype(F32)
-        total = total + xrecv[4 - 2 * zh, rows].astype(F32) + xrecv[3 + 2 * zh, rows].astype(F32)
-        zh_copy[q].wait_recv()
-        out_w[rows] = total + zhrecv[rows].astype(F32)
-
-    for p in all_parts:
-        total = R[y, zl, :, pl.ds(p * PART, PART)].astype(F32)
-        for j in range(1, NZ):
-            zs = (zl + j) % NZ
-            pltpu.make_async_remote_copy(
-                src_ref=zrecv.at[p, zs],
-                dst_ref=zrecv.at[p, zs],
-                send_sem=send_sem.at[z_live[p] + zs],
-                recv_sem=recv_sem.at[z_live[p] + zs],
-                device_id=at(zl=zs),
-                device_id_type=MESH,
-            ).wait_recv()
-            total = total + zrecv[p, zs].astype(F32)
-        out_rows[:, pl.ds(p * PART, PART)] = total.astype(BF16)
-
+        for step in (2, 3):
+            for plus in (True, False):
+                t_copy(step, q, plus).wait_recv()
+        zhsend[x_rows_of(q)] = x_total(1 - zh, x_rows_of(q)).astype(BF16)
+        begin(zh_copy(q))
+
+    def write(rows, total):
+        out_w[rows] = total
+        one = pltpu.make_async_copy(out_w.at[rows], w_hbm.at[rows], load_sem.at[len(written)])
+        one.start()
+        written.append(one)
+
+    def x_final(q):
+        rows = x_rows_of(q)
+        total = x_total(zh, rows)
+        zh_copy(q).wait_recv()
+        write(rows, total + zhrecv[rows].astype(F32))
+
+    z_rows = pl.ds(X_ROWS, Z_ROWS)
+    z_half = [pl.ds(X_ROWS, Z_ROWS // 2), pl.ds(X_ROWS + Z_ROWS // 2, Z_ROWS // 2)]
+
+    def zw_copy(n):
+        src = t_ref(x_order[n], 1 - zh, z_rows)
+        return copy(src, zwrecv.at[n], other_run, sem_of(("zw", n)))
+
+    def z_add(n):
+        zw_copy(n).wait_recv()
+        ref = t_ref(x_order[n], zh, z_rows)
+        ref[...] = add(ref, zwrecv[n]).astype(BF16)
+
+    def h_copy(step, plus):
+        xx, half = {
+            (1, True): (x2, 0), (1, False): (x2, 1), (2, True): (x1, 1),
+            (2, False): (x3, 0), (3, True): (x1, 0), (3, False): (x3, 1),
+        }[step, plus]
+        slot = 2 * (step - 1) + (0 if plus else 1)
+        src = t_ref(xx, zh, z_half[half])
+        return copy(src, hrecv.at[slot], right if plus else left, sem_of(("h", step, plus)))
+
+    def h_turn(plus):
+        h_copy(1, plus).wait_recv()
+        ref = t_ref(x1, zh, z_half[0]) if plus else t_ref(x3, zh, z_half[1])
+        ref[...] = add(ref, hrecv[0 if plus else 1]).astype(BF16)
+        begin(h_copy(3, plus))
+
+    def h_final():
+        for step in (2, 3):
+            for plus in (True, False):
+                h_copy(step, plus).wait_recv()
+        low = add(t_ref(x, zh, z_half[0]), hrecv[4], hrecv[3])
+        high = add(t_ref(x, zh, z_half[1]), hrecv[2], hrecv[5])
+        write(z_rows, jnp.concatenate([low, high], axis=0))
+
+    for code in AFTER:
+        kind, p, q, r = code // 1000, code // 100 % 10, code // 10 % 10, code % 10
+        if kind == 10:
+            weight_grad(block_of(x_order[p], q, 1 - c))
+            begin(core_copy(p, q))
+        elif kind == 11:
+            row_grad(p)
+        elif kind == 12:
+            weight_grad(block_of(x_order[p], q, c))
+        elif kind == 13:
+            core_sum(p, q)
+        elif kind in (14, 15):
+            begin(t_copy(kind - 13, p, q == 1))
+        elif kind == 16:
+            x_turn(p, q == 1)
+        elif kind == 17:
+            x_end(p)
+        elif kind == 18:
+            x_final(p)
+        elif kind == 19:
+            r_step(p, q, r == 1)
+        elif kind == 20:
+            r_end(p)
+        elif kind == 21:
+            r_final(p)
+        elif kind == 22:
+            begin(zw_copy(p))
+        elif kind == 23:
+            z_add(p)
+        elif kind in (24, 25):
+            begin(h_copy(kind - 23, p == 1))
+        elif kind == 26:
+            h_turn(p == 1)
+        else:
+            h_final()
+
+    one = pltpu.make_async_copy(out_rows, rows_hbm, load_sem.at[len(written)])
+    one.start()
+    written.append(one)
+    for one in written:
+        one.wait()
     for one in sent:
         one.wait_send()
     for key in y_keys:
@@ -523,9 +583,13 @@
             jax.ShapeDtypeStruct((2 * CAP, D // 2), BF16),
             jax.ShapeDtypeStruct((3 * UNITS, COLS), F32),
         ),
-        in_specs=[hbm, hbm, vmem, vmem, hbm, hbm],
-        out_specs=(vmem, vmem),
+        in_specs=[hbm] * 6,
+        out_specs=(hbm, hbm),
         scratch_shapes=[
+            pltpu.VMEM(routes.shape, routes.dtype),
+            pltpu.VMEM(router_probs.shape, F32),
+            pltpu.VMEM((2 * CAP, D // 2), BF16),
+            pltpu.VMEM((3 * UNITS, COLS), F32),
             pltpu.VMEM((n_tok, D), BF16),
             pltpu.VMEM((n_tok, D), BF16),
             pltpu.VMEM((blocks, 2 * CAP, D), BF16),
@@ -537,10 +601,12 @@
             pltpu.VMEM((PARTS, NZ, 2 * CAP, PART), BF16),
             pltpu.VMEM((16, 3 * UNITS, COLS), BF16),
             pltpu.VMEM((8, 3 * UNITS, COLS), BF16),
-            pltpu.VMEM((6, 3 * UNITS, COLS), BF16),
-            pltpu.VMEM((3 * UNITS, COLS), BF16),
-            pltpu.VMEM((3 * UNITS, COLS), BF16),
-            pltpu.SemaphoreType.DMA((5,)),
+            pltpu.VMEM((6, X_ROWS, COLS), BF16),
+            pltpu.VMEM((X_ROWS, COLS), BF16),
+            pltpu.VMEM((X_ROWS, COLS), BF16),
+            pltpu.VMEM((4, Z_ROWS, COLS), BF16),
+            pltpu.VMEM((6, Z_ROWS // 2, COLS), BF16),
+            pltpu.SemaphoreType.DMA((7,)),
             pltpu.SemaphoreType.DMA((n_sems,)),
             pltpu.SemaphoreType.DMA((n_sems,)),
         ],

time: 95.6 us -> 90.5 us (0.947)
  Pallas kernels: 94.1 us -> 89.7 us
    pallas_call x1, Pallas kernels: 91 us -> 86.7 us  [on_device(): pl.pallas_call(kernel, out_shape=(jax.ShapeDtypeStruct((2 * CAP, D // 2),...]
where the time goes in v3:
time: 90.5 us; the launch traced here: 90.4 us
  Pallas kernels  89.7 us (99%)
    pallas_call x1, Pallas kernels, on_device(): pl.pallas_call(kernel, out_shape=(jax.ShapeDtypeStruct((2 * CAP, D // 2),...  86.7 us
    pallas_call x1, Pallas kernels, on_device(): pl.pallas_call(finish, out_shape=(jax.ShapeDtypeStruct(tokens_in.shape, B...  3.04 us

profile of v3, /device:TPU:1, one launch (start us, length us, event | category | flops | bytes accessed | tf_op | source)
XLA Modules:
  0.0 90.4 jit_solution(14386705758442852792)
XLA Ops:
  0.6 86.7 %expert_backward.1 = (bf16[16,2048]{1,0:T(8,128)(2,1)}, f32[384,256]{1,0:T(8,128)}) custom-call(bf16[128,4096]{1,0:T(8,128)(2,1)} %tok_hbm.1, bf16[128,4096]{1,0:T(8,128)(2,1)} %og_hbm.1, s32[2,128]{1,0:T(2,128)} %bitcast.2, f32[2,128]{1,0:T(2,128)} %bitcast.4, bf16[2,128,256]{2,1,0:T(8,128)(2,1)} %gu_hbm.1, bf16[128,256]{1,0:T(8,128)(2,1)} %dn_hbm.1), custom_call_target="tpu_custom_call" | custom-call | flops 6000000000 | bytes 4194304 | tf_op jit(solution)/shard_map/expert_backward/pallas_call | solution.py:580
  87.3 3.0 %finish.1 = (bf16[128,4096]{1,0:T(8,128)(2,1)}, f32[2,128,256]{2,1,0:T(8,128)}, f32[128,256]{1,0:T(8,128)}) custom-call(s32[2,128]{1,0:T(2,128)} %bitcast.3, f32[2,128]{1,0:T(2,128)} %bitcast.5, bf16[16,2048]{1,0:T(8,128)(2,1)} %get-tuple-element.5.rows_hbm, f32[384,256]{1,0:T(8,128)} %get-tuple-element.6.grads_hbm), custom_call_target="tpu_custom_call" | custom-call | tf_op jit(solution)/shard_map/finish/pallas_call | solution.py:621

commit v4 on v3

--- a/solution.py
+++ b/solution.py
@@ -68,14 +68,18 @@
     return picker, jnp.sum(picker * weight, axis=1, keepdims=True)
 
 
+N_SEND, N_RECV = 14, 158
+
+
 class Sems:
-    def __init__(self, send, recv):
-        self.send, self.recv, self.used = send, recv, 0
-
-    def take(self, n=1):
-        at = self.used
-        self.used += n
-        return at
+    def __init__(self):
+        self.named, self.used = {}, 0
+
+    def __call__(self, name, n=1):
+        if name not in self.named:
+            self.named[name] = self.used
+            self.used += n
+        return self.named[name]
 
 
 def kernel(
@@ -133,48 +137,39 @@
 
     pl.semaphore_wait(barrier, len(peers))
 
-    sems = Sems(send_sem, recv_sem)
-    sent = []
-
-    def copy(src, dst, device, k):
+    sent, due = Sems(), Sems()
+
+    def copy(src, dst, device, group, k):
         return pltpu.make_async_remote_copy(
             src_ref=src,
             dst_ref=dst,
-            send_sem=send_sem.at[k],
+            send_sem=send_sem.at[sent(group)],
             recv_sem=recv_sem.at[k],
             device_id=device,
             device_id_type=MESH,
         )
 
-    def go(src, dst, device, k=None):
-        one = copy(src, dst, device, sems.take() if k is None else k)
-        one.start()
-        sent.append(one)
-        return one
+    def all_sent(group, ref):
+        copy(ref, ref, other_core, group, 0).wait_send()
+
+    def all_due(k, ref):
+        copy(ref, ref, other_core, "rows", k).wait_recv()
 
     upper = zl // 2
     m = zl * (1 - upper) + (3 - zl) * upper
     order = [b * (1 - upper) + (3 - b) * upper for b in (m, 1 - m, 2, 3)]
 
     col_parts = [pl.ds(0, FIRST), pl.ds(FIRST, FIRST), pl.ds(2 * FIRST, D - 2 * FIRST)]
-    held = {}
-
-    def sem_of(key, n=1):
-        if key not in held:
-            held[key] = sems.take(n)
-        return held[key]
 
     def z_copy(part, d, zs, up):
         ref = G.at[(y + d) % NY * NZ + zs, :, col_parts[part]]
-        to_send = sem_of(("up" if up else "down", part, d), NZ)
-        return pltpu.make_async_remote_copy(
-            src_ref=ref,
-            dst_ref=ref,
-            send_sem=send_sem.at[to_send + zs],
-            recv_sem=recv_sem.at[sem_of(("up", part, d), NZ) + zs],
-            device_id=at(zl=(zl + (1 if up else NZ - 1)) % NZ),
-            device_id_type=MESH,
-        )
+        to = (zl + (1 if up else NZ - 1)) % NZ
+        k = due(("z", part, d), NZ - 1) + (zs - to + 2 * NZ - 1) % NZ
+        return copy(ref, ref, at(zl=to), ("z", part), k)
+
+    def z_due(part, d, zs):
+        ref = G.at[(y + d) % NY * NZ + zs, :, col_parts[part]]
+        return copy(ref, ref, north, ("z", part), due(("z", part, d), NZ - 1) + (zs - zl + 2 * NZ - 1) % NZ)
 
     def z_both(act, part, d, zs):
         @pl.when((zs <= zl) & (zl < NZ - 1))
@@ -194,7 +189,7 @@
     def y_copy(part, k, h, plus):
         src_y = (y + (NY - h + 1 if plus else h - 1)) % NY
         ref = G.at[src_y * NZ + order[k], :, col_parts[part]]
-        return copy(ref, ref, north if plus else south, sem_of(("y", part, k, h, plus)))
+        return copy(ref, ref, north if plus else south, ("y", part), due(("y", part, k, h, plus)))
 
     def block_of(xx, zz, cc):
         return (xx * 2 + zz) * 2 + cc
@@ -208,22 +203,19 @@
 
     def to_core(n, xx):
         ref = w_ref(xx, runs[n])
-        return copy(ref, ref, other_core, sem_of(("core", n, [xx is one for one in (x, x1, x2, x3)].index(True))))
+        return copy(ref, ref, other_core, "weights", due("core"))
 
     def to_run():
-        return copy(w_ref(x, zh), w_ref(x, zh), other_run, sem_of("run"))
+        return copy(w_ref(x, zh), w_ref(x, zh), other_run, "weights", due("w_run"))
 
     def x_copy(n, hop, plus):
         if hop == 1:
             ref = w_ref(x, runs[n])
         else:
             ref = w_ref(x3, runs[n], lo) if plus else w_ref(x1, runs[n], hi)
-        return copy(ref, ref, right if plus else left, sem_of(("x", n, hop, plus)))
+        return copy(ref, ref, right if plus else left, "weights", due(("x", n, hop, plus)))
 
     y_keys = [(p, k, h, plus) for p in range(3) for k in range(4 if p < 2 else 1) for plus in (True, False) for h in range(1, hops(k, plus) + 1)]
-    z_keys = [(p, d, k) for p in range(3) for d in range(1 if p < 2 else NY) for k in range(4)]
-    x_keys = [(n, hop, plus) for n in range(2) for hop in (1, 2) for plus in (True, False)]
-    core_keys = [(n, xx) for n in range(2) for xx in (x, x1, x2, x3)]
 
     def exchange(codes):
         taken = set()
@@ -237,7 +229,7 @@
             take(lambda: y_copy(*key), "y", *key)
 
         def take_z(p, d, k):
-            take(lambda: z_copy(p, d, order[k], True), "z", p, d, k)
+            take(lambda: z_due(p, d, order[k]), "z", p, d, k)
 
         for code in codes:
             kind, p, q, r, w = (code // 10**e % 10 for e in (4, 3, 2, 1, 0))
@@ -271,11 +263,10 @@
                 to_core(p, x2).start()
         for key in y_keys:
             take_y(*key)
-        for key in core_keys:
-            to_core(*key).wait_recv()
+        all_due(due("core"), W.at[:, pl.ds(0, 8 * COLS)])
 
     for key in y_keys:
-        sem_of(("y", *key))
+        due(("y", *key))
 
     @pl.when((zl == 0) | (zl == NZ - 1))
     def _():
@@ -318,7 +309,6 @@
 
     def begin(one):
         one.start()
-        sent.append(one)
 
     def add(ref, *terms):
         total = ref[...].astype(F32)
@@ -328,7 +318,7 @@
 
     def core_copy(n, zz):
         i = block_of(x_order[n], zz, 1 - c)
-        return copy(T.at[i], crecv.at[2 * n + zz], other_core, sem_of(("c", n, zz)))
+        return copy(T.at[i], crecv.at[2 * n + zz], other_core, "cores", due(("c", n, zz)))
 
     def core_sum(n, zz):
         core_copy(n, zz).wait_recv()
@@ -353,7 +343,7 @@
 
     def r_copy(p, s, plus):
         src, dst = r_part(r_dest(p, s, plus), p), yrecv.at[r_slot[p, s, plus]]
-        return copy(src, dst, north if plus else south, sem_of(("r", p, s, plus)))
+        return copy(src, dst, north if plus else south, "row_sums", due(("r", p, s, plus)))
 
     def r_step(p, s, plus):
         r_copy(p, s, plus).wait_recv()
@@ -372,16 +362,9 @@
         for plus in (True, False):
             begin(r_copy(p, 1, plus))
 
-    def run_copy(p, zs, arriving):
-        base = sem_of(("run", p), NZ)
-        return pltpu.make_async_remote_copy(
-            src_ref=R.at[y, zs, :, pl.ds(p * PART, PART)],
-            dst_ref=zrecv.at[p, zs if arriving else zl],
-            send_sem=send_sem.at[base + zs],
-            recv_sem=recv_sem.at[base + (zs if arriving else zl)],
-            device_id=at(zl=zs),
-            device_id_type=MESH,
-        )
+    def run_copy(p, zs):
+        src = R.at[y, zs, :, pl.ds(p * PART, PART)]
+        return copy(src, zrecv.at[p, zl], at(zl=zs), "rows", due(("run", p)))
 
     def r_end(p):
         ways = (True, False)
@@ -391,12 +374,11 @@
         terms = [yrecv[r_slot[p, r_hops(p, plus), plus]] for plus in ways]
         ref[...] = add(ref, *terms).astype(BF16)
         for j in range(1, NZ):
-            begin(run_copy(p, (zl + j) % NZ, False))
+            begin(run_copy(p, (zl + j) % NZ))
 
     def r_final(p):
         others = [(zl + j) % NZ for j in range(1, NZ)]
-        for zs in others:
-            run_copy(p, zs, True).wait_recv()
+        all_due(due(("run", p)), zrecv.at[p, pl.ds(0, NZ - 1)])
         here = pl.ds(p * PART, PART)
         total = add(R.at[y, zl, :, here], *[zrecv[p, zs] for zs in others])
         out_rows[:, here] = total.astype(BF16)
@@ -414,7 +396,8 @@
         }[step, plus]
         slot = 2 * (step - 1) + (0 if plus else 1)
         src, dst = t_ref(xx, zz, x_rows_of(q)), xrecv.at[slot, x_rows_of(q)]
-        return copy(src, dst, right if plus else left, sem_of(("t", step, q, plus)))
+        k = due(("t", q, plus) if step == 1 else ("t", q))
+        return copy(src, dst, right if plus else left, "round_x", k)
 
     def x_turn(q, plus):
         t_copy(1, q, plus).wait_recv()
@@ -427,12 +410,10 @@
 
     def zh_copy(q):
         rows = x_rows_of(q)
-        return copy(zhsend.at[rows], zhrecv.at[rows], other_run, sem_of(("zh", q)))
+        return copy(zhsend.at[rows], zhrecv.at[rows], other_run, "sums", due(("zh", q)))
 
     def x_end(q):
-        for step in (2, 3):
-            for plus in (True, False):
-                t_copy(step, q, plus).wait_recv()
+        all_due(due(("t", q)), xrecv.at[pl.ds(0, 4), x_rows_of(0)])
         zhsend[x_rows_of(q)] = x_total(1 - zh, x_rows_of(q)).astype(BF16)
         begin(zh_copy(q))
 
@@ -453,7 +434,7 @@
 
     def zw_copy(n):
         src = t_ref(x_order[n], 1 - zh, z_rows)
-        return copy(src, zwrecv.at[n], other_run, sem_of(("zw", n)))
+        return copy(src, zwrecv.at[n], other_run, "to_run", due(("zw", n)))
 
     def z_add(n):
         zw_copy(n).wait_recv()
@@ -467,7 +448,8 @@
         }[step, plus]
         slot = 2 * (step - 1) + (0 if plus else 1)
         src = t_ref(xx, zh, z_half[half])
-        return copy(src, hrecv.at[slot], right if plus else left, sem_of(("h", step, plus)))
+        k = due(("h", plus) if step == 1 else "h")
+        return copy(src, hrecv.at[slot], right if plus else left, "halves", k)
 
     def h_turn(plus):
         h_copy(1, plus).wait_recv()
@@ -476,9 +458,7 @@
         begin(h_copy(3, plus))
 
     def h_final():
-        for step in (2, 3):
-            for plus in (True, False):
-                h_copy(step, plus).wait_recv()
+        all_due(due("h"), hrecv.at[pl.ds(0, 4)])
         low = add(t_ref(x, zh, z_half[0]), hrecv[4], hrecv[3])
         high = add(t_ref(x, zh, z_half[1]), hrecv[2], hrecv[5])
         write(z_rows, jnp.concatenate([low, high], axis=0))
@@ -524,17 +504,30 @@
     written.append(one)
     for one in written:
         one.wait()
-    for one in sent:
-        one.wait_send()
-    for key in y_keys:
-        y_copy(*key).wait_send()
-    for p, d, k in z_keys:
-        z_both(lambda one: one.wait_send(), p, d, order[k])
-    for key in x_keys:
-        x_copy(*key).wait_send()
-    for key in core_keys:
-        to_core(*key).wait_send()
-    to_run().wait_send()
+    for part in range(3):
+        all_sent(("y", part), G.at[pl.ds(0, 28 if part < 2 else 7), :, col_parts[part]])
+
+    @pl.when((zl == 0) | (zl == NZ - 1))
+    def _():
+        for part in range(3):
+            all_sent(("z", part), G.at[pl.ds(0, 1 if part < 2 else NY), :, col_parts[part]])
+
+    @pl.when((zl > 0) & (zl < NZ - 1))
+    def _():
+        for part in range(2):
+            all_sent(("z", part), G.at[pl.ds(0, 5), :, col_parts[part]])
+        all_sent(("z", 2), G.at[pl.ds(0, 20), :, pl.ds(0, 2 * (D - 2 * FIRST))])
+
+    all_sent("weights", W.at[:, pl.ds(0, 15 * COLS)])
+    all_sent("cores", T.at[pl.ds(0, 8)])
+    all_sent("row_sums", yrecv)
+    all_sent("rows", zrecv.at[pl.ds(0, PARTS * (NZ - 1) // NZ)])
+    all_sent("round_x", xrecv)
+    all_sent("sums", zhsend)
+    all_sent("to_run", zwrecv)
+    all_sent("halves", hrecv)
+    if (sent.used, due.used) != (N_SEND, N_RECV):
+        raise ValueError(f"{sent.used} {due.used}")
 
 
 def finish(routes, probs, rows_hbm, grads_hbm, out_tok, out_gu, out_dn, rows, grads, buf, sem):
@@ -575,7 +568,6 @@
     hbm = pl.BlockSpec(memory_space=pltpu.HBM)
     n_tok = tokens_in.shape[0]
     blocks = NY * NZ
-    n_sems = 320
     routes, router_probs = routes.T, router_probs.T
     rows, grads = pl.pallas_call(
         kernel,
@@ -607,8 +599,8 @@
             pltpu.VMEM((4, Z_ROWS, COLS), BF16),
             pltpu.VMEM((6, Z_ROWS // 2, COLS), BF16),
             pltpu.SemaphoreType.DMA((7,)),
-            pltpu.SemaphoreType.DMA((n_sems,)),
-            pltpu.SemaphoreType.DMA((n_sems,)),
+            pltpu.SemaphoreType.DMA((N_SEND,)),
+            pltpu.SemaphoreType.DMA((N_RECV,)),
         ],
         compiler_params=pltpu.CompilerParams(
             collective_id=0, has_side_effects=True, vmem_limit_bytes=56 * 2**20

time: 90.5 us -> 86 us (0.950)
  Pallas kernels: 89.7 us -> 85.2 us
    pallas_call x1, Pallas kernels: 86.7 us -> 82.2 us  [on_device(): pl.pallas_call(kernel, out_shape=(jax.ShapeDtypeStruct((2 * CAP, D // 2),...]
where the time goes in v4:
time: 86 us; the launch traced here: 85.8 us
  Pallas kernels  85.2 us (99%)
    pallas_call x1, Pallas kernels, on_device(): pl.pallas_call(kernel, out_shape=(jax.ShapeDtypeStruct((2 * CAP, D // 2),...  82.2 us
    pallas_call x1, Pallas kernels, on_device(): pl.pallas_call(finish, out_shape=(jax.ShapeDtypeStruct(tokens_in.shape, B...  3.04 us

profile of v4, /device:TPU:1, one launch (start us, length us, event | category | flops | bytes accessed | tf_op | source)
XLA Modules:
  0.0 85.8 jit_solution(11606221345607731349)
XLA Ops:
  0.6 82.2 %expert_backward.1 = (bf16[16,2048]{1,0:T(8,128)(2,1)}, f32[384,256]{1,0:T(8,128)}) custom-call(bf16[128,4096]{1,0:T(8,128)(2,1)} %tok_hbm.1, bf16[128,4096]{1,0:T(8,128)(2,1)} %og_hbm.1, s32[2,128]{1,0:T(2,128)} %bitcast.2, f32[2,128]{1,0:T(2,128)} %bitcast.4, bf16[2,128,256]{2,1,0:T(8,128)(2,1)} %gu_hbm.1, bf16[128,256]{1,0:T(8,128)(2,1)} %dn_hbm.1), custom_call_target="tpu_custom_call" | custom-call | flops 6000000000 | bytes 4194304 | tf_op jit(solution)/shard_map/expert_backward/pallas_call | solution.py:572
  82.8 3.0 %finish.1 = (bf16[128,4096]{1,0:T(8,128)(2,1)}, f32[2,128,256]{2,1,0:T(8,128)}, f32[128,256]{1,0:T(8,128)}) custom-call(s32[2,128]{1,0:T(2,128)} %bitcast.3, f32[2,128]{1,0:T(2,128)} %bitcast.5, bf16[16,2048]{1,0:T(8,128)(2,1)} %get-tuple-element.5.rows_hbm, f32[384,256]{1,0:T(8,128)} %get-tuple-element.6.grads_hbm), custom_call_target="tpu_custom_call" | custom-call | tf_op jit(solution)/shard_map/finish/pallas_call | solution.py:613

commit v5 on v4

--- a/solution.py
+++ b/solution.py
@@ -31,24 +31,24 @@
     21000, 21200, 21300,
 )
 AT_ENDS = (
-    11010, 21000, 11011, 20000, 12010, 10011, 10010, 12011, 40000, 30000, 11111, 11110, 11021, 11020,
-    22100, 10111, 10110, 12021, 12020, 10021, 10020, 22000, 21010, 11121, 11120, 20010, 50000, 11031,
-    11030, 10121, 50100, 22600, 22200, 10120, 12031, 12030, 10031, 22700, 10030, 11130, 21020, 11211,
-    11210, 22110, 11041, 20020, 10211, 11131, 10210, 60000, 22010, 41000, 10130, 22500, 12041, 10041,
-    11140, 10131, 22300, 11220, 10220, 11221, 10140, 22710, 11311, 22210, 11310, 22400, 11230, 10311,
-    20030, 10221, 21030, 10310, 22020, 22120, 22720, 22610, 22220, 11231, 11321, 10230, 10321, 51100,
-    11320, 11240, 51000, 10231, 10240, 10320, 11331, 22310, 22030, 22620, 10331, 61000, 11330, 11341,
-    22530, 22510, 22130, 10341, 10330, 22430, 22630, 22320, 22420, 22730, 22230, 22330, 22410, 22520,
+    21000, 12010, 11010, 11011, 20000, 10010, 12011, 40000, 10011, 30000, 11110, 12020, 11111, 22100,
+    11021, 10110, 11020, 10111, 10021, 22000, 12021, 50100, 10020, 20010, 11121, 11120, 11031, 22200,
+    11030, 10121, 22600, 10120, 50000, 12031, 21010, 12030, 11130, 22700, 10031, 11210, 11211, 22110,
+    10030, 11131, 21020, 10211, 10130, 10210, 22500, 22300, 10131, 60000, 12041, 11041, 11221, 11140,
+    11220, 41000, 10140, 10220, 10041, 11311, 11310, 10311, 11230, 22010, 22120, 10221, 22400, 20020,
+    22220, 11231, 22020, 22720, 21030, 10310, 11321, 22610, 10230, 20030, 22210, 10321, 11320, 51100,
+    22620, 51000, 11240, 10320, 11331, 22510, 22710, 10331, 22310, 22730, 11330, 22230, 10240, 10231,
+    22530, 11341, 61000, 22030, 10330, 10341, 22130, 22520, 22410, 22420, 22330, 22320, 22430, 22630,
 )
 INSIDE = (
-    21000, 11011, 11010, 20000, 12011, 12010, 10011, 10010, 40000, 11210, 11021, 30000, 21020, 21010,
-    11211, 11111, 20010, 20020, 11110, 10021, 11020, 10211, 10111, 10110, 10210, 22100, 22000, 22700,
-    11220, 12020, 50100, 50000, 12021, 11221, 11120, 11031, 11121, 11030, 12031, 22200, 21030, 10020,
-    10221, 10120, 11311, 22600, 11310, 10220, 10311, 22020, 10031, 10121, 60000, 10310, 11231, 11130,
-    22110, 20030, 22710, 11131, 22610, 22220, 12030, 22720, 22010, 11041, 22120, 10030, 22310, 11230,
-    22620, 11320, 10231, 22210, 11321, 22510, 41000, 12041, 22500, 10131, 22130, 10041, 22300, 10230,
-    10320, 22030, 22730, 11140, 10321, 22410, 22530, 10130, 22320, 51000, 22230, 11330, 10330, 11240,
-    51100, 11331, 22520, 22330, 10140, 22400, 10331, 22630, 10240, 11341, 22430, 61000, 10341, 22420,
+    21000, 11011, 11010, 12010, 40000, 20000, 12011, 10011, 10010, 11021, 11111, 11210, 30000, 11020,
+    21010, 21020, 11211, 20010, 20020, 10021, 10111, 10210, 22100, 11110, 50000, 10211, 22000, 12020,
+    22700, 12021, 11120, 11031, 11221, 10110, 10020, 11220, 11121, 22200, 22600, 11030, 50100, 10121,
+    21030, 11310, 12031, 11311, 10311, 10310, 10221, 22020, 12030, 20030, 10120, 22120, 22110, 11231,
+    10031, 22710, 22220, 11131, 11130, 22010, 60000, 22720, 22210, 11320, 22310, 10220, 11041, 10231,
+    11230, 22620, 11321, 22510, 22130, 22730, 22500, 41000, 12041, 10030, 10320, 22300, 10131, 10230,
+    22610, 22230, 22030, 22530, 10041, 10321, 10130, 22320, 11331, 10330, 22410, 51100, 51000, 22400,
+    22330, 10240, 11140, 10331, 22520, 11240, 11330, 11341, 22430, 10140, 22420, 61000, 22630, 10341,
 )
 
 

time: 86 us -> 85.6 us (level)
  Pallas kernels: 85.2 us -> 84.3 us
    pallas_call x1, Pallas kernels: 82.2 us -> 81.3 us  [on_device(): pl.pallas_call(kernel, out_shape=(jax.ShapeDtypeStruct((2 * CAP, D // 2),...]
where the time goes in v5:
time: 85.6 us; the launch traced here: 85 us
  Pallas kernels  84.3 us (98%)
    pallas_call x1, Pallas kernels, on_device(): pl.pallas_call(kernel, out_shape=(jax.ShapeDtypeStruct((2 * CAP, D // 2),...  81.3 us
    pallas_call x1, Pallas kernels, on_device(): pl.pallas_call(finish, out_shape=(jax.ShapeDtypeStruct(tokens_in.shape, B...  3.04 us

profile of v5, /device:TPU:1, one launch (start us, length us, event | category | flops | bytes accessed | tf_op | source)
XLA Modules:
  0.0 85.0 jit_solution(12046164025367972165)
XLA Ops:
  0.6 81.3 %expert_backward.1 = (bf16[16,2048]{1,0:T(8,128)(2,1)}, f32[384,256]{1,0:T(8,128)}) custom-call(bf16[128,4096]{1,0:T(8,128)(2,1)} %tok_hbm.1, bf16[128,4096]{1,0:T(8,128)(2,1)} %og_hbm.1, s32[2,128]{1,0:T(2,128)} %bitcast.2, f32[2,128]{1,0:T(2,128)} %bitcast.4, bf16[2,128,256]{2,1,0:T(8,128)(2,1)} %gu_hbm.1, bf16[128,256]{1,0:T(8,128)(2,1)} %dn_hbm.1), custom_call_target="tpu_custom_call" | custom-call | flops 6000000000 | bytes 4194304 | tf_op jit(solution)/shard_map/expert_backward/pallas_call | solution.py:572
  81.9 3.0 %finish.1 = (bf16[128,4096]{1,0:T(8,128)(2,1)}, f32[2,128,256]{2,1,0:T(8,128)}, f32[128,256]{1,0:T(8,128)}) custom-call(s32[2,128]{1,0:T(2,128)} %bitcast.3, f32[2,128]{1,0:T(2,128)} %bitcast.5, bf16[16,2048]{1,0:T(8,128)(2,1)} %get-tuple-element.5.rows_hbm, f32[384,256]{1,0:T(8,128)} %get-tuple-element.6.grads_hbm), custom_call_target="tpu_custom_call" | custom-call | tf_op jit(solution)/shard_map/finish/pallas_call | solution.py:613
